TPU v7x, 512 devices: a whole 4x8x8 slice. The times are simulated.
512 devices in a mesh: tensor: 8 (over y), near: 2 (over z_hi), far: 32 (over z_lo, x, core).
Axes of the slice: x: 4, y: 8, z: 8 (z_hi: 2, z_lo: 4; z = z_hi * 4 + z_lo), core: 2. Of those that a mesh axis runs over, the one named last changes fastest.
Arguments:
- grad_output: bfloat16 [8192, 2304], P(('near', 'far')), may hold values from -6 to 6
- layer_input: bfloat16 [2, 8192, 2304], P(None, ('near', 'far'), 'tensor'), may hold values from -16 to 16
- norm_gain: float32 [2, 2304], replicated, may hold values from 0.5 to 2
- queries: bfloat16 [2, 8192, 2048], P(None, ('near', 'far'), 'tensor'), may hold values from -6 to 6
- keys: bfloat16 [2, 8192, 1024], P(None, ('near', 'far'), 'tensor'), may hold values from -6 to 6
- value_weight: bfloat16 [2, 2304, 1024], P(None, None, 'tensor'), may hold values from -0.125 to 0.125
- output_weight: bfloat16 [2, 2048, 2304], P(None, 'tensor', 'near'), may hold values from -0.125 to 0.125
Outputs:
- grad_input: bfloat16 [8192, 2304], P(('near', 'far'), 'tensor')
- grad_value_weight: float32 [2, 2304, 1024], P(None, ('near', 'far'), 'tensor')
- grad_norm_gain: float32 [2, 2304], P(None, 'tensor')
All inputs are finite; a program needn't handle non-finite values.
Results may differ from a plain program's by a relative error of at most 0.023.
Values may be sent and summed in bfloat16 or wider, within the bound.
A program may use at most 64 MiB of HBM per device.

v0:
```python
import math

import jax
import jax.numpy as jnp
from jax import lax
from jax.sharding import PartitionSpec as P

HD = 128


softcap = 50.0
query_scale = 1.0 / 12.0


def value_gradient(query_block, key_block, context_grad):
    length = query_block.shape[0]
    query_pos = lax.broadcasted_iota(jnp.int32, (2 * length, length), 0) % length
    key_pos = lax.broadcasted_iota(jnp.int32, (2 * length, length), 1)
    causal = key_pos <= query_pos
    query_pair = jnp.concatenate([query_block[:, 0:HD], query_block[:, HD : 2 * HD]], 0)
    grad_pair = jnp.concatenate([context_grad[:, 0:HD], context_grad[:, HD : 2 * HD]], 0)
    scores = lax.dot_general(
        query_pair, key_block, (((1,), (1,)), ((), ())), preferred_element_type=jnp.float32
    )
    capped = softcap * jnp.tanh(scores * query_scale / softcap)
    weights = jnp.where(causal, jnp.exp(capped), 0.0)
    probs = (weights / jnp.sum(weights, axis=1, keepdims=True)).astype(jnp.bfloat16)
    spread = lax.dot_general(
        probs, grad_pair, (((0,), (0,)), ((), ())), preferred_element_type=jnp.float32
    )
    results = spread.astype(jnp.bfloat16)
    return results


def body(grad_output, layer_input, norm_gain, queries, keys, value_weight, output_weight):
    tokens = grad_output.shape[0]
    layers = layer_input.shape[0]
    token_total = tokens * lax.axis_size("near") * lax.axis_size("far")
    norm_scale = 1.0 / math.sqrt(token_total)
    feat_local = layer_input.shape[2]
    feature_start = lax.axis_index("tensor") * feat_local
    inputs = lax.all_gather(layer_input, "tensor", axis=2, tiled=True)
    cotangent = grad_output
    final_share = lax.dynamic_slice_in_dim(grad_output, feature_start, feat_local, 1)
    weight_grads = [None] * layers
    gain_grads = [None] * layers
    for depth_index in reversed(range(layers)):
        rows_full = inputs[depth_index].astype(jnp.float32)
        inverse = lax.rsqrt(jnp.mean(rows_full * rows_full, axis=1, keepdims=True) + 1e-06)
        normed = rows_full * inverse
        gain = norm_gain[depth_index]
        scaled_input = (normed * gain).astype(jnp.bfloat16)
        current = cotangent
        context_grad = lax.dot_general(
            current,
            lax.all_gather(output_weight[depth_index], "near", axis=1, tiled=True),
            (((1,), (1,)), ((), ())),
            preferred_element_type=jnp.float32,
        ).astype(jnp.bfloat16)
        value_grad = value_gradient(queries[depth_index], keys[depth_index], context_grad)
        term = (
            lax.dot_general(
                scaled_input,
                value_grad,
                (((0,), (0,)), ((), ())),
                preferred_element_type=jnp.float32,
            )
            * norm_scale
        )
        weight_grads[depth_index] = lax.psum_scatter(
            term, ("near", "far"), scatter_dimension=0, tiled=True
        )
        partial_term = lax.dot_general(
            value_grad,
            value_weight[depth_index],
            (((1,), (1,)), ((), ())),
            preferred_element_type=jnp.float32,
        )
        summed = lax.psum(partial_term.astype(jnp.bfloat16), "tensor").astype(jnp.float32)
        gated = summed * gain
        mixed = jnp.mean(gated * normed, axis=1, keepdims=True)
        input_grad = inverse * (gated - normed * mixed)
        gain_full = jnp.sum(summed * normed, axis=0) * norm_scale
        gain_grads[depth_index] = lax.dynamic_slice_in_dim(gain_full, feature_start, feat_local, 0)
        cotangent = (cotangent.astype(jnp.float32) + input_grad).astype(jnp.bfloat16)
        final_share = lax.dynamic_slice_in_dim(cotangent, feature_start, feat_local, 1)
    gain_stack = lax.psum(jnp.stack(gain_grads), ("near", "far"))
    return (final_share, jnp.stack(weight_grads), gain_stack)


def solution(mesh):
    return jax.shard_map(
        body,
        mesh=mesh,
        in_specs=(
            P(("near", "far"), None),
            P(None, ("near", "far"), "tensor"),
            P(),
            P(None, ("near", "far"), "tensor"),
            P(None, ("near", "far"), "tensor"),
            P(None, None, "tensor"),
            P(None, "tensor", "near"),
        ),
        out_specs=(
            P(("near", "far"), "tensor"),
            P(None, ("near", "far"), "tensor"),
            P(None, "tensor"),
        ),
        check_vma=False,
    )
```

profile of v0, /device:TPU:1, one launch (start us, length us, event | category | flops | bytes accessed | tf_op | source)
XLA Modules:
  0.0 522.4 jit_solution(12442280581841769994)
XLA Ops:
  7.2 0.0 copy-start.4
  7.2 0.0 copy-start.7
  7.2 0.0 all-gather.8.cloned.1.call-start
  7.2 2.4 fusion.70
  9.7 0.0 all-gather.8.cloned.1.call-update
  9.7 0.0 all-gather.6.cloned.1.call-start
  9.7 0.0 copy-done.4
  9.7 0.8 copy.13
  10.5 0.0 all-gather.6.cloned.1.call-update
  10.5 0.0 all-reduce.7.cloned.1.call-start
  10.6 0.0 copy-done.7
  10.7 0.0 copy-done.10
  10.7 0.2 fusion.75
  10.9 0.0 copy-start.2
  10.9 52.7 %all-gather.8.cloned.1.call-done = bf16[1,256,2304]{2,1,0:T(8,128)(2,1)} async-done(((bf16[1,256,1152]{2,1,0:T(8,128)(2,1)}), bf16[1,256,2304]{2,1,0:T(8,128)(2,1)}) %all-gather.8.cloned.1.call-update) | async-done | bytes 1179664 | tf_op jit(solution)/shard_map/all_gather | solution.py:56
  63.6 0.0 copy-done
  63.6 1.8 fusion.26
  65.4 0.1 convolution_convert_fusion.3
  65.6 0.0 copy-start.5
  65.6 0.6 copy-done.5
  66.2 0.0 copy-done.2
  66.2 1.1 convolution_convert_fusion.1
  67.3 0.0 all-reduce.7.cloned.1.call-update
  67.4 0.0 all-gather.10.cloned.1.call-start
  67.4 0.5 all-gather.10.cloned.1.call-update
  67.9 0.0 all-reduce.9.cloned.1.call-start
  68.0 0.0 copy-done.9
  68.0 0.6 slice_reduce_fusion
  68.6 0.8 fusion.76
  69.5 29.7 %all-gather.6.cloned.1.call-done = bf16[2,128,2304]{1,0,2:T(2,128)(2,1)} async-done(((bf16[2,128,288]{1,0,2:T(2,128)(2,1)}), bf16[2,128,2304]{1,0,2:T(2,128)(2,1)}) %all-gather.6.cloned.1.call-update) | async-done | bytes 1179664 | tf_op jit(solution)/shard_map/all_gather | solution.py:42
  99.1 3.7 fusion.69
  102.9 1.5 copy.18
  104.4 0.2 fusion.12
  104.7 74.4 %all-reduce.7.cloned.1.call-done = bf16[128,2304]{1,0:T(8,128)(2,1)} async-done(((bf16[128,2304]{1,0:T(8,128)(2,1)}), bf16[128,2304]{1,0:T(8,128)(2,1)}) %all-reduce.7.cloned.1.call-update) | async-done | bytes 589840 | tf_op jit(solution)/shard_map/psum | solution.py:79
  179.0 1.6 fusion.11
  180.6 0.0 copy-done.1
  180.6 0.5 fusion.7
  181.1 0.0 copy-start.11
  181.1 51.2 %all-gather.10.cloned.1.call-done = bf16[1,256,2304]{2,1,0:T(8,128)(2,1)} async-done(((bf16[1,256,1152]{2,1,0:T(8,128)(2,1)}), bf16[1,256,2304]{2,1,0:T(8,128)(2,1)}) %all-gather.10.cloned.1.call-update) | async-done | bytes 1179664 | tf_op jit(solution)/shard_map/all_gather | solution.py:56
  232.3 1.9 fusion.29
  234.2 0.1 convolution_convert_fusion.2
  234.4 0.0 copy-done.3
  234.4 1.2 convolution_convert_fusion
  235.6 0.0 all-reduce.9.cloned.1.call-update
  235.6 0.0 all-reduce.11.cloned.1.call-start
  235.6 0.0 copy-start.6
  235.6 1.5 copy.19
  237.2 0.0 copy-start.8
  237.2 0.2 fusion.13
  237.4 1.5 convolution_multiply_fusion
  238.9 1.5 convolution_multiply_fusion.1
  240.3 0.0 all-reduce.11.cloned.1.call-update
  240.3 1.3 dynamic-slice
  242.3 0.1 dynamic-slice_multiply_fusion.1
  242.4 64.1 %all-reduce.9.cloned.1.call-done = bf16[128,2304]{1,0:T(8,128)(2,1)} async-done(((bf16[128,2304]{1,0:T(8,128)(2,1)}), bf16[128,2304]{1,0:T(8,128)(2,1)}) %all-reduce.9.cloned.1.call-update) | async-done | bytes 589840 | tf_op jit(solution)/shard_map/psum | solution.py:79
  306.5 1.5 fusion.8
  308.0 0.2 fusion.45
  308.2 0.7 copy.16
  309.0 0.1 dynamic-slice_multiply_fusion.2
  309.1 130.5 %psum.23 = f32[2,288]{1,0:T(2,128)} all-reduce(f32[2,288]{1,0:T(2,128)S(1)} %pad_maximum_fusion.1), channel_id=1, replica_groups=mesh['tensor'=8,'near'=2,'far'=32] {'near','far'}, use_global_device_ids=true, to_apply=%region_12.13 | all-reduce | flops 576 | bytes 4608 | tf_op jit(solution)/shard_map/psum | solution.py:87
  439.6 73.8 %all-reduce.11.cloned.1.call-done = (f32[2304,128]{1,0:T(8,128)}, f32[2304,128]{1,0:T(8,128)}) async-done(((f32[2304,128]{1,0:T(8,128)}, f32[2304,128]{1,0:T(8,128)}), (f32[2304,128]{1,0:T(8,128)}, f32[2304,128]{1,0:T(8,128)})) %all-reduce.11.cloned.1.call-update) | async-done | bytes 2359312
  513.4 0.7 dynamic-slice_bitcast_fusion
  514.1 0.7 dynamic-slice_bitcast_fusion.1
  514.9 0.6 copy.17
  (22 shorter events, 0.1 us)
Async XLA Ops:
  7.2 2.6 copy-start.4
  7.2 3.4 copy-start.7
  7.2 56.4 %all-gather.8.cloned.1.call-start = ((), (), s32[]{:S(2)}) async-start(), calls=%async_computation.3 | async-start | bytes 1769472 | tf_op jit(solution)/shard_map/all_gather | solution.py:56
  9.7 1.0 copy-start.10
  9.7 53.9 %copy-start = (bf16[128,2304]{1,0:T(8,128)(2,1)S(1)}, bf16[128,2304]{1,0:T(8,128)(2,1)}, u32[]{:S(2)}) copy-start(bf16[128,2304]{1,0:T(8,128)(2,1)} %param.7) | copy-start | bytes 1769476
  9.7 89.5 %all-gather.6.cloned.1.call-start = ((), (), s32[]{:S(2)}) async-start(), calls=%async_computation | async-start | bytes 1327104 | tf_op jit(solution)/shard_map/all_gather | solution.py:42
  10.5 168.5 %all-reduce.7.cloned.1.call-start = ((), (), s32[]{:S(2)}) async-start(), calls=%async_computation.1 | async-start | bytes 1179648 | tf_op jit(solution)/shard_map/psum | solution.py:79
  10.9 55.3 %copy-start.2 = (bf16[2,2304,128]{2,1,0:T(8,128)(2,1)S(1)}, bf16[2,2304,128]{2,1,0:T(8,128)(2,1)}, u32[]{:S(2)}) copy-start(bf16[2,2304,128]{2,1,0:T(8,128)(2,1)} %param.12) | copy-start | bytes 3538948
  65.6 0.6 copy-start.5
  66.2 1.8 copy-start.9
  67.4 164.9 %all-gather.10.cloned.1.call-start = ((), (), s32[]{:S(2)}) async-start(), calls=%async_computation.4 | async-start | bytes 1769472 | tf_op jit(solution)/shard_map/all_gather | solution.py:56
  67.9 238.5 %all-reduce.9.cloned.1.call-start = ((), (), s32[]{:S(2)}) async-start(), calls=%async_computation.2 | async-start | bytes 1179648 | tf_op jit(solution)/shard_map/psum | solution.py:79
  179.0 1.6 copy-start.1
  181.1 53.1 %copy-start.11 = (f32[256,128]{0,1:T(8,128)S(1)}, f32[256,128]{0,1:T(8,128)}, u32[]{:S(2)}) copy-start(f32[256,128]{0,1:T(8,128)} %get-tuple-element.36) | copy-start | bytes 393220
  232.3 2.1 copy-start.3
  235.6 277.8 %all-reduce.11.cloned.1.call-start = ((), (), s32[]{:S(2)}) async-start(), calls=%async_computation.5 | async-start | bytes 4718592
  235.6 1.8 copy-start.6
  237.2 1.7 copy-start.8
Sparse Core Ops, SparseCore 0:
  10.1 53.4 all-gather.7
  65.7 33.4 all-gather.5
  101.5 77.4 all-reduce.6
  181.0 51.2 all-gather.9
  235.7 70.7 all-reduce.8
  309.8 203.5 all-reduce.10
where the time goes:
time: 524 us; the launch traced here: 522 us
  waiting for transfers between devices  346 us (66%)
  blocking collectives  131 us (25%)
  local copies, waits for them, and re-layouts  15.5 us (3%)
  between operations  15 us (3%)
  matrix products  10.3 us (2%)
    psum x2, waiting for transfers between devices, body(): lax.psum(partial_term.astype(jnp.bfloat16), 'tensor').astype(jnp.float32)  139 us
    psum x1, blocking collectives, body(): gain_stack = lax.psum(jnp.stack(gain_grads), ('near', 'far'))  131 us
    all_gather x2, waiting for transfers between devices, body(): lax.all_gather(output_weight[depth_index], 'near', axis=1, tiled=True)  104 us
    unnamed x7, waiting for transfers between devices  74.4 us
    all_gather x1, waiting for transfers between devices, body(): inputs = lax.all_gather(layer_input, 'tensor', axis=2, tiled=True)  29.7 us
  transfers between devices with their start and end apart: 6, of which 6 were waited for; matrix products, arithmetic and copies ran while one was open for 4% of the time, Pallas kernels for 0%

commit v1 on v0

v1 whole, which is shorter than its diff:
```python
import math

import jax
import jax.numpy as jnp
from jax import lax
from jax.experimental import pallas as pl
from jax.experimental.pallas import tpu as pltpu
from jax.sharding import PartitionSpec as P

MESH = pl.DeviceIdType.MESH
F32 = jnp.float32
BF = jnp.bfloat16

N = 8
TOK = 128
HD = 128
FB = 288
D = 2304
HALF = 1152
ROWS = 36
FAR_FIRST = (4, 3, 5, 2, 6, 1, 7)


def nt(a, b):
    return lax.dot_general(a, b, (((1,), (1,)), ((), ())), preferred_element_type=F32)


def nn(a, b):
    return lax.dot_general(a, b, (((1,), (0,)), ((), ())), preferred_element_type=F32)


def wrap(i):
    return lax.rem(i, N)


def device(y, z, g):
    return (y, z // 4, lax.rem(z, 4) * 8 + g)


def column_to_row(col):
    return jnp.transpose(jnp.broadcast_to(col, (TOK, TOK)))[0:8]


def row_to_column(row):
    return jnp.transpose(jnp.broadcast_to(row, (TOK, TOK)))


def kernel(
    cot, x, gain, q, k, vw, wo,
    out, dw_out, gain_out,
    xt, pad, gvt, probs, wot, mrx, mz, mt, vb, xn, sq, dvy, dva, mm, gx, gz, dwf, dws, dwr, cot_blk, gain_blk, inv_row, inv_col,
    sq_s, sq_r, xt_s, xt_r, sw_s, sw_r, wz_s, wz_r, wx_s, wx_r, mz_s, mz_r, mt_s, mt_r, vb_s, vb_r, xn_s, xn_r,
    dvy_s, dvy_r, dva_s, dva_r, mm_s, mm_r, gx_s, gx_r, gz_s, gz_r, dw_s, dw_r,
):
    scale = 1.0 / math.sqrt(8192.0)
    y = lax.axis_index("tensor")
    data = lax.axis_index("near") * 32 + lax.axis_index("far")
    z = data // N
    g = lax.rem(data, N)
    near = z // 4
    core = lax.rem(g, 2)
    sib = g + 1 - 2 * core

    def on_y(i):
        return device(i, z, g)

    def on_z(i):
        return device(y, i, g)

    def on_g(i):
        return device(y, z, i)

    def copy(src, dst, ss, rs, dev):
        return pltpu.make_async_remote_copy(
            src_ref=src, dst_ref=dst, send_sem=ss, recv_sem=rs, device_id=dev, device_id_type=MESH
        )

    def gather_start(buf, me, ss, rs, dev):
        for n in FAR_FIRST:
            copy(buf.at[me], buf.at[me], ss.at[n], rs.at[me], dev(wrap(me + n))).start()

    def gather_wait(buf, me, ss, rs, dev):
        for n in (1, 7, 2, 6, 3, 5, 4):
            slot = wrap(me + n)
            copy(buf.at[slot], buf.at[slot], ss.at[n], rs.at[slot], dev(slot)).wait_recv()

    def gather_sent(buf, me, ss, rs, dev):
        for n in range(1, N):
            copy(buf.at[me], buf.at[me], ss.at[n], rs.at[me], dev(wrap(me + n))).wait_send()

    def chip_start(buf, ss, rs):
        for n in (4, 2, 6):
            copy(buf.at[g], buf.at[g], ss.at[n], rs.at[g], on_g(wrap(g + n))).start()
        copy(buf.at[g], buf.at[g], ss.at[1], rs.at[g], on_g(sib)).start()

    def chip_pass(buf, ss, rs):
        for n in (2, 6, 4):
            slot = wrap(g + n)
            copy(buf.at[slot], buf.at[slot], ss.at[n], rs.at[slot], on_g(slot)).wait_recv()
            copy(buf.at[slot], buf.at[slot], ss.at[n + 1], rs.at[slot], on_g(sib)).start()

    def chip_wait(buf, ss, rs):
        for n in (0, 2, 6, 4):
            slot = wrap(sib + n)
            copy(buf.at[slot], buf.at[slot], ss.at[1], rs.at[slot], on_g(sib)).wait_recv()

    def chip_sent(buf, ss, rs):
        for n in range(1, N):
            copy(buf.at[g], buf.at[g], ss.at[n], rs.at[g], on_g(sib)).wait_send()

    barrier = pltpu.get_barrier_semaphore()

    def hello(dev):
        pl.semaphore_signal(barrier, inc=1, device_id=dev, device_id_type=MESH)

    for n in FAR_FIRST:
        hello(on_y(wrap(y + n)))
        hello(on_z(wrap(z + n)))
        hello(on_g(wrap(g + n)))
    swap_self = y == g

    @pl.when(jnp.logical_not(swap_self))
    def _():
        hello(device(g, z, y))

    plane_self = jnp.logical_and(y == z, g == y)
    for n in range(N):
        at_self = jnp.logical_and(plane_self, z == n)

        @pl.when(jnp.logical_not(at_self))
        def _():
            hello(device(z, jnp.int32(n), y))

    sq[y] = jnp.zeros((8, TOK), F32)
    pad[...] = jnp.zeros((TOK, 384), F32)
    for l in (0, 1):
        xf = x[l].astype(F32)
        sq[y, l : l + 1, :] = column_to_row(jnp.sum(xf * xf, axis=1, keepdims=True))[0:1]
    pad[:, 0:FB] = x[1].astype(F32)
    xt[y, 0:128, :] = jnp.transpose(pad[:, 0:128]).astype(BF)
    xt[y, 128:256, :] = jnp.transpose(pad[:, 128:256]).astype(BF)
    xt[y, 256:288, :] = jnp.transpose(pad[:, 256:384])[0:32].astype(BF)
    for i in range(D // 128):
        part = jnp.transpose(vw[1, 128 * i : 128 * i + 128, :].astype(F32))
        gvt[:, 128 * i : 128 * i + 128] = (part * gain[1:2, 128 * i : 128 * i + 128]).astype(BF)
    for b in range(N):

        @pl.when(y == b)
        def _():
            cot_blk[...] = cot[:, FB * b : FB * b + FB].astype(F32)
            gain_blk[...] = gain[:, FB * b : FB * b + FB]

    pl.semaphore_wait(
        barrier, 3 * (N - 1) + 1 + N - swap_self.astype(jnp.int32) - plane_self.astype(jnp.int32)
    )

    mirror = 7 - z
    rows32 = pl.multiple_of(32 * g, 32)

    def wo_chunk(l):
        return copy(
            wo.at[l, pl.ds(rows32, 32), :], wot.at[l, g], wz_s.at[l], wz_r.at[l], on_z(mirror)
        )

    def swap_slice():
        return gvt.at[
            pl.ds(pl.multiple_of(32 * lax.rem(z, 4), 32), 32), pl.ds(pl.multiple_of(HALF * near, 128), HALF)
        ]

    def swap_block():
        return vw.at[:, pl.ds(pl.multiple_of(FB * g, 16), FB), :]

    partner = device(g, z, y)
    wo_chunk(1).start()
    gather_start(sq, y, sq_s, sq_r, on_y)

    @pl.when(jnp.logical_not(swap_self))
    def _():
        copy(swap_slice(), mrx, sw_s.at[0], sw_r.at[0], partner).start()

    @pl.when(swap_self)
    def _():
        pltpu.make_async_copy(swap_slice(), mrx, sw_r.at[0]).start()

    wo_chunk(0).start()

    @pl.when(jnp.logical_not(swap_self))
    def _():
        copy(swap_block(), vb.at[y], sw_s.at[1], sw_r.at[1], partner).start()

    @pl.when(swap_self)
    def _():
        pltpu.make_async_copy(swap_block(), vb.at[y], sw_r.at[1]).start()

    gather_start(xt, y, xt_s, xt_r, on_y)

    causal = lax.broadcasted_iota(jnp.int32, (TOK, TOK), 0) <= lax.broadcasted_iota(jnp.int32, (TOK, TOK), 1)
    for l in (1, 0):
        for h in (0, 1):
            scores = nt(k[l], q[l, :, HD * h : HD * h + HD])
            weights = jnp.where(causal, jnp.exp(50.0 * jnp.tanh(scores * (1.0 / 600.0))), 0.0)
            probs[2 * l + h] = (weights / jnp.sum(weights, axis=0, keepdims=True)).astype(BF)

    mine = pl.ds(pl.multiple_of(HALF * near, 128), HALF)
    other = pl.ds(pl.multiple_of(HALF * (1 - near), 128), HALF)
    dctx1 = nt(wo[1], cot[:, mine])

    wo_chunk(1).wait_recv()
    chip_start(wot.at[1], wx_s.at[1], wx_r.at[1])

    copy(mrx, mrx, sw_s.at[0], sw_r.at[0], partner).wait_recv()
    mz[z] = nt(mrx[...], wo[0]).astype(BF)
    gather_start(mz, z, mz_s, mz_r, on_z)

    wo_chunk(0).wait_recv()
    chip_start(wot.at[0], wx_s.at[0], wx_r.at[0])

    gather_wait(sq, y, sq_s, sq_r, on_y)
    total = sq[0]
    for n in range(1, N):
        total = total + sq[n]
    inv_row[...] = lax.rsqrt(total * (1.0 / D) + 1e-6)
    for l in (0, 1):
        inv_col[l] = row_to_column(inv_row[l : l + 1, :])
        pad[:, 0:FB] = x[l].astype(F32) * inv_col[l][:, 0:1] * gain_blk[l : l + 1, :]
        xn[g, l, 0:128, :] = jnp.transpose(pad[:, 0:128]).astype(BF)
        xn[g, l, 128:256, :] = jnp.transpose(pad[:, 128:256]).astype(BF)
        xn[g, l, 256:288, :] = jnp.transpose(pad[:, 256:384])[0:32].astype(BF)

    chip_pass(wot.at[1], wx_s.at[1], wx_r.at[1])
    chip_wait(wot.at[1], wx_s.at[1], wx_r.at[1])

    def values(l, dctx):
        return nt(probs[2 * l], dctx[0:HD]) + nt(probs[2 * l + 1], dctx[HD : 2 * HD])

    dctx1 = (dctx1 + nt(wot[1].reshape(2 * HD, HALF), cot[:, other])).astype(BF)
    dvy[1, y] = values(1, dctx1).astype(BF)
    gather_start(dvy.at[1], y, dvy_s.at[1], dvy_r.at[1], on_y)
    dv1_t = nt(dctx1[0:HD], probs[2]) + nt(dctx1[HD : 2 * HD], probs[3])

    gather_wait(mz, z, mz_s, mz_r, on_z)
    m_sum = mz[0:4].reshape(HD, 2 * HD).astype(F32) + mz[4:8].reshape(HD, 2 * HD).astype(F32)
    mt[g] = jnp.transpose(m_sum).astype(BF)
    chip_start(mt, mt_s, mt_r)

    chip_pass(wot.at[0], wx_s.at[0], wx_r.at[0])
    chip_wait(wot.at[0], wx_s.at[0], wx_r.at[0])
    chip_start(xn, xn_s, xn_r)
    copy(swap_block(), vb.at[g], sw_s.at[1], sw_r.at[1], partner).wait_recv()
    chip_start(vb, vb_s, vb_r)
    wo_other = wot[0].reshape(2 * HD, HALF)
    base = nt(wo[0], cot[:, mine]) + nt(wo_other, cot[:, other])

    gather_wait(xt, y, xt_s, xt_r, on_y)
    u_t = nn(gvt[...], xt[...].reshape(D, TOK))
    part = jnp.sum(dv1_t.astype(BF).astype(F32) * u_t, axis=0, keepdims=True)
    mm[1, y] = jnp.broadcast_to(part, (8, TOK))
    gather_start(mm.at[1], y, mm_s.at[1], mm_r.at[1], on_y)
    xt_half = [xt[0:4].reshape(HALF, TOK), xt[4:8].reshape(HALF, TOK)]
    first = near == 0
    xt_mine = jnp.where(first, xt_half[0], xt_half[1])
    xt_other = jnp.where(first, xt_half[1], xt_half[0])
    y1 = nn(wo[0], xt_mine) + nn(wo_other, xt_other)

    chip_pass(mt, mt_s, mt_r)
    chip_wait(mt, mt_s, mt_r)

    def pass_heads(l):
        for n in (0, 1, 7, 2, 6, 3, 5, 4):
            head = wrap(y + n)
            if n > 0:
                copy(dvy.at[l, head], dvy.at[l, head], dvy_s.at[l, n], dvy_r.at[l, head], on_y(head)).wait_recv()

            @pl.when(head != g)
            def _():
                copy(dvy.at[l, head], dva.at[l, g], dva_s.at[l, head], dva_r.at[l, g], on_g(head)).start()

            @pl.when(head == g)
            def _():
                dva[l, g] = dvy[l, head]

    def heads_wait(l):
        for n in (1, 2, 7, 6, 3, 5, 4):
            slot = wrap(g + n)
            copy(dva.at[l, slot], dva.at[l, slot], dva_s.at[l, slot], dva_r.at[l, slot], on_g(slot)).wait_recv()

    def heads_sent(l):
        for n in range(1, N):
            slot = wrap(g + n)
            copy(dvy.at[l, slot], dva.at[l, g], dva_s.at[l, slot], dva_r.at[l, g], on_g(slot)).wait_send()

    pass_heads(1)
    corr = nt(mt[0], dvy[1, 0])
    for n in range(1, N):
        corr = corr + nt(mt[n], dvy[1, n])
    gather_wait(mm.at[1], y, mm_s.at[1], mm_r.at[1], on_y)
    total = mm[1, 0]
    for n in range(1, N):
        total = total + mm[1, n]
    inv1 = inv_row[1:2, :]
    mean1 = inv1 * total[0:1, :] * (1.0 / D)
    dctx0 = (base + inv1 * (corr - (inv1 * mean1) * y1)).astype(BF)
    dvy[0, y] = values(0, dctx0).astype(BF)
    gather_start(dvy.at[0], y, dvy_s.at[0], dvy_r.at[0], on_y)

    def scatter(l, n, start):
        at_self = jnp.logical_and(plane_self, g == n)
        away = copy(dws.at[l, n], dwr.at[l, z], dw_s.at[l, n], dw_r.at[l, z], device(g, y, jnp.int32(n)))

        @pl.when(jnp.logical_not(at_self))
        def _():
            if start:
                away.start()
            else:
                away.wait_send()

        if start:

            @pl.when(at_self)
            def _():
                pltpu.make_async_copy(dws.at[l, n], dwr.at[l, z], dw_r.at[l, z]).start()

    def weight_grad(l):
        block = nn(xn[0, l], dva[l, 0])
        for n in range(1, N):
            block = block + nn(xn[n, l], dva[l, n])
        dwf[...] = block * scale
        for n in range(N):
            dws[l, n, 0:ROWS, :] = dwf[ROWS * n : ROWS * n + ROWS, :]
            dws[l, n, ROWS:40, :] = jnp.zeros((40 - ROWS, HD), F32)
            scatter(l, n, True)

    def weight_sum(l):
        for n in range(N):
            copy(dwr.at[l, n], dwr.at[l, n], dw_s.at[l, n], dw_r.at[l, n], partner).wait_recv()
        block = dwr[l, 0]
        for n in range(1, N):
            block = block + dwr[l, n]
        dw_out[l] = block[0:ROWS]

    def input_grad(l):
        dxn = nt(dvy[l, 0], vb[0, l])
        for n in range(1, N):
            dxn = dxn + nt(dvy[l, n], vb[n, l])
        xhat = x[l].astype(F32) * inv_col[l][:, 0:1]
        gx[g, l : l + 1, 0:FB] = jnp.sum(dxn * xhat, axis=0, keepdims=True) * scale
        return xhat, dxn * gain_blk[l : l + 1, :]

    chip_pass(xn, xn_s, xn_r)
    chip_wait(xn, xn_s, xn_r)
    chip_pass(vb, vb_s, vb_r)
    chip_wait(vb, vb_s, vb_r)
    heads_wait(1)
    weight_grad(1)
    gx[g] = jnp.zeros((8, 384), F32)
    xhat, gg = input_grad(1)
    cot_blk[...] = (
        (cot_blk[...] + inv_col[1][:, 0:1] * (gg - xhat * row_to_column(mean1)[:, 0:1])).astype(BF).astype(F32)
    )

    pass_heads(0)
    xhat, gg = input_grad(0)
    mm[0, y] = column_to_row(jnp.sum(gg * xhat, axis=1, keepdims=True) * (1.0 / D))
    gather_start(mm.at[0], y, mm_s.at[0], mm_r.at[0], on_y)
    gather_start(gx, g, gx_s, gx_r, on_g)
    heads_wait(0)
    weight_grad(0)

    gather_wait(gx, g, gx_s, gx_r, on_g)
    total = gx[0]
    for n in range(1, N):
        total = total + gx[n]
    gz[z] = total
    gather_start(gz, z, gz_s, gz_r, on_z)

    gather_wait(mm.at[0], y, mm_s.at[0], mm_r.at[0], on_y)
    total = mm[0, 0]
    for n in range(1, N):
        total = total + mm[0, n]
    mean0 = row_to_column(total[0:1, :])[:, 0:1]
    out[...] = (cot_blk[...] + inv_col[0][:, 0:1] * (gg - xhat * mean0)).astype(BF)

    weight_sum(1)
    gather_wait(gz, z, gz_s, gz_r, on_z)
    total = gz[0]
    for n in range(1, N):
        total = total + gz[n]
    gain_out[...] = total[0:2, 0:FB]
    weight_sum(0)

    gather_sent(sq, y, sq_s, sq_r, on_y)
    gather_sent(xt, y, xt_s, xt_r, on_y)
    gather_sent(mz, z, mz_s, mz_r, on_z)
    gather_sent(gx, g, gx_s, gx_r, on_g)
    gather_sent(gz, z, gz_s, gz_r, on_z)
    chip_sent(mt, mt_s, mt_r)
    chip_sent(vb, vb_s, vb_r)
    chip_sent(xn, xn_s, xn_r)
    for l in (0, 1):
        wo_chunk(l).wait_send()
        chip_sent(wot.at[l], wx_s.at[l], wx_r.at[l])
        gather_sent(dvy.at[l], y, dvy_s.at[l], dvy_r.at[l], on_y)
        gather_sent(mm.at[l], y, mm_s.at[l], mm_r.at[l], on_y)
        heads_sent(l)
        for n in range(N):
            scatter(l, n, False)

    @pl.when(jnp.logical_not(swap_self))
    def _():
        copy(swap_slice(), mrx, sw_s.at[0], sw_r.at[0], partner).wait_send()
        copy(swap_block(), vb.at[y], sw_s.at[1], sw_r.at[1], partner).wait_send()


def body(grad_output, layer_input, norm_gain, queries, keys, value_weight, output_weight):
    vmem = pltpu.VMEM
    dma = pltpu.SemaphoreType.DMA
    one = [dma((N,)), dma((N,))]
    two = [dma((2, N)), dma((2, N))]
    pair = [dma((2,)), dma((2,))]
    return pl.pallas_call(
        kernel,
        out_shape=(
            jax.ShapeDtypeStruct((TOK, FB), BF),
            jax.ShapeDtypeStruct((2, ROWS, HD), F32),
            jax.ShapeDtypeStruct((2, FB), F32),
        ),
        in_specs=[pl.BlockSpec(memory_space=vmem)] * 7,
        out_specs=[pl.BlockSpec(memory_space=vmem)] * 3,
        scratch_shapes=[
            vmem((N, FB, TOK), BF),
            vmem((TOK, 384), F32),
            vmem((HD, D), BF),
            vmem((4, TOK, TOK), BF),
            vmem((2, N, 32, HALF), BF),
            vmem((32, HALF), BF),
            vmem((N, 32, 2 * HD), BF),
            vmem((N, 2 * HD, HD), BF),
            vmem((N, 2, FB, HD), BF),
            vmem((N, 2, FB, TOK), BF),
            vmem((N, 8, TOK), F32),
            vmem((2, N, TOK, HD), BF),
            vmem((2, N, TOK, HD), BF),
            vmem((2, N, 8, TOK), F32),
            vmem((N, 8, 384), F32),
            vmem((N, 8, 384), F32),
            vmem((FB, HD), F32),
            vmem((2, N, 40, HD), F32),
            vmem((2, N, 40, HD), F32),
            vmem((TOK, FB), F32),
            vmem((2, FB), F32),
            vmem((8, TOK), F32),
            vmem((2, TOK, TOK), F32),
        ]
        + one
        + one
        + pair
        + pair
        + two
        + one
        + one
        + one
        + one
        + two
        + two
        + two
        + one
        + one
        + two,
        compiler_params=pltpu.CompilerParams(
            collective_id=0, has_side_effects=True, vmem_limit_bytes=48 * 2**20
        ),
    )(grad_output, layer_input, norm_gain, queries, keys, value_weight, output_weight)


def solution(mesh):
    return jax.shard_map(
        body,
        mesh=mesh,
        in_specs=(
            P(("near", "far"), None),
            P(None, ("near", "far"), "tensor"),
            P(),
            P(None, ("near", "far"), "tensor"),
            P(None, ("near", "far"), "tensor"),
            P(None, None, "tensor"),
            P(None, "tensor", "near"),
        ),
        out_specs=(
            P(("near", "far"), "tensor"),
            P(None, ("near", "far"), "tensor"),
            P(None, "tensor"),
        ),
        check_vma=False,
    )
```

time: 524 us -> 122 us (0.23)
  waiting for transfers between devices: 346 us -> 0 us
  blocking collectives: 131 us -> 0 us
  Pallas kernels: 0 us -> 112 us
  between operations: 15 us -> 0.66 us
  matrix products: 10.3 us -> 0 us
  local copies, waits for them, and re-layouts: 15.5 us -> 9.09 us
    psum x2 -> x0, waiting for transfers between devices: 139 us -> none  [body(): lax.psum(partial_term.astype(jnp.bfloat16), 'tensor').astype(jnp.float32)]
    all_gather x3 -> x0, waiting for transfers between devices: 134 us -> none  [the longest x2 104 us: body(): lax.all_gather(output_weight[depth_index], 'near', axis=1, tiled=True)]
    psum x1 -> x0, blocking collectives: 131 us -> none  [body(): gain_stack = lax.psum(jnp.stack(gain_grads), ('near', 'far'))]
    pallas_call x0 -> x1, Pallas kernels: none -> 112 us  [body(): pl.pallas_call(kernel, out_shape=(jax.ShapeDtypeStruct((TOK, FB), BF), ja...]
    unnamed x7 -> x0, waiting for transfers between devices: 74.4 us -> none
    dot_general x10 -> x0, matrix products: 10.3 us -> none  [the longest x2 3.72 us: body(): lax.dot_general(current, lax.all_gather(output_weight[depth_index], 'near...]
    slice x6 -> x0, local copies, waits for them, and re-layouts: 6.84 us -> none  [the longest x1 3.75 us: body(): rows_full = inputs[depth_index].astype(jnp.float32)]
  transfers between devices with their start and end apart: 6 -> 0, of which waited for: 6 -> 0; matrix products, arithmetic and copies ran while one was open for 4% -> 0% of each run, Pallas kernels for 0% -> 0%
where the time goes in v1:
time: 122 us
  Pallas kernels  112 us (92%)
  local copies, waits for them, and re-layouts  9.09 us (7%)
    pallas_call x1, Pallas kernels, body(): pl.pallas_call(kernel, out_shape=(jax.ShapeDtypeStruct((TOK, FB), BF), ja...  112 us
    unnamed x14, local copies, waits for them, and re-layouts  7.71 us

profile of v1, /device:TPU:1, one launch (start us, length us, event | category | flops | bytes accessed | tf_op | source)
XLA Modules:
  0.0 122.1 jit_solution(1773239406114964768)
XLA Ops:
  0.6 1.1 copy.10.x
  1.7 0.0 copy-start
  1.7 1.3 %copy-done = bf16[2,2304,128]{2,1,0:T(8,128)(2,1)S(1)} copy-done((bf16[2,2304,128]{2,1,0:T(8,128)(2,1)S(1)}, bf16[2,2304,128]{2,1,0:T(8,128)(2,1)}, u32[]{:S(2)}) %copy-start) | copy-done | bytes 1179672
  3.0 0.0 copy-start.1
  3.0 1.3 %copy-done.1 = bf16[2,256,1152]{2,1,0:T(8,128)(2,1)S(1)} copy-done((bf16[2,256,1152]{2,1,0:T(8,128)(2,1)S(1)}, bf16[2,256,1152]{2,1,0:T(8,128)(2,1)}, u32[]{:S(2)}) %copy-start.1) | copy-done | bytes 1179672
  4.3 0.0 copy-start.2
  4.3 1.1 copy-done.2
  5.3 0.0 copy-start.3
  5.3 0.9 copy-done.3
  6.2 0.0 copy-start.4
  6.2 0.8 copy-done.4
  7.1 0.0 copy-start.5
  7.1 0.7 copy-done.5
  7.8 112.3 %shard_map.94 = (bf16[128,288]{1,0:T(8,128)(2,1)S(1)}, f32[2,36,128]{2,1,0:T(8,128)S(1)}, f32[2,288]{1,0:T(2,128)S(1)}) custom-call(bf16[128,2304]{1,0:T(8,128)(2,1)S(1)} %copy-done.2, bf16[2,128,288]{2,1,0:T(8,128)(2,1)S(1)} %copy.10.x, f32[2,2304]{1,0:T(2,128)S(1)} %copy-done.5, bf16[2,128,256]{2,1,0:T(8,128)(2,1)S(1)} %copy-done.3, ...), custom_call_target="tpu_custom_call" | custom-call | tf_op jit(solution)/shard_map/pallas_call | solution.py:420
  120.1 0.7 copy.11
  120.9 0.6 copy.12
  121.5 0.6 copy.14
Async XLA Ops:
  1.7 1.3 %copy-start = (bf16[2,2304,128]{2,1,0:T(8,128)(2,1)S(1)}, bf16[2,2304,128]{2,1,0:T(8,128)(2,1)}, u32[]{:S(2)}) copy-start(bf16[2,2304,128]{2,1,0:T(8,128)(2,1)} %vw.1) | copy-start | bytes 3538948
  3.0 1.3 %copy-start.1 = (bf16[2,256,1152]{2,1,0:T(8,128)(2,1)S(1)}, bf16[2,256,1152]{2,1,0:T(8,128)(2,1)}, u32[]{:S(2)}) copy-start(bf16[2,256,1152]{2,1,0:T(8,128)(2,1)} %wo.1) | copy-start | bytes 3538948
  4.3 1.1 copy-start.2
  5.3 0.9 copy-start.3
  6.2 0.8 copy-start.4
  7.1 0.7 copy-start.5

commit v2 on v0

v2 whole, which is shorter than its diff:
```python
import math

import jax
import jax.numpy as jnp
from jax import lax
from jax.experimental import pallas as pl
from jax.experimental.pallas import tpu as pltpu
from jax.sharding import PartitionSpec as P

MESH = pl.DeviceIdType.MESH
F32 = jnp.float32
BF = jnp.bfloat16

N = 8
TOK = 128
HD = 128
FB = 288
D = 2304
HALF = 1152
ROWS = 36
FAR_FIRST = (4, 3, 5, 2, 6, 1, 7)
NEAR_FIRST = (1, 7, 2, 6, 3, 5, 4)


def nt(a, b):
    return lax.dot_general(a, b, (((1,), (1,)), ((), ())), preferred_element_type=F32)


def nn(a, b):
    return lax.dot_general(a, b, (((1,), (0,)), ((), ())), preferred_element_type=F32)


def wrap(i):
    return lax.rem(i, N)


def device(y, z, g):
    return (y, z // 4, lax.rem(z, 4) * 8 + g)


def sum_of(ref):
    total = ref[0]
    for n in range(1, N):
        total = total + ref[n]
    return total


def kernel(
    cot_in, x_in, gain_in, q_in, k_in, vw_in, wo_in,
    out, dw_out, gain_out,
    cot, gain, q, k, vw, wo,
    xt, gcol, gvt, probs, wot, mrx, mz, mt, vb, xnb, xnf, xnp, xna, dvy, dva, mm, gys, gy, gx, gz, dwf, dws, dwr, pad, cot_blk, gain_blk, inv_row,
    in_r, xt_s, xt_r, sw_s, sw_r, wz_s, wz_r, wx_s, wx_r, mz_s, mz_r, mt_s, mt_r, vb_s, vb_r, xn_s, xn_r,
    dvy_s, dvy_r, dva_s, dva_r, mm_s, mm_r, gy_s, gy_r, gx_s, gx_r, gz_s, gz_r, dw_s, dw_r,
):
    scale = 1.0 / math.sqrt(8192.0)
    y = lax.axis_index("tensor")
    data = lax.axis_index("near") * 32 + lax.axis_index("far")
    z = data // N
    g = lax.rem(data, N)
    near = z // 4
    core = lax.rem(g, 2)
    sib = g + 1 - 2 * core

    def on_y(i):
        return device(i, z, g)

    def on_z(i):
        return device(y, i, g)

    def on_g(i):
        return device(y, z, i)

    def copy(src, dst, ss, rs, dev):
        return pltpu.make_async_remote_copy(
            src_ref=src, dst_ref=dst, send_sem=ss, recv_sem=rs, device_id=dev, device_id_type=MESH
        )

    under_way = []

    class Gather:
        def __init__(self, buf, me, sems, dev):
            self.buf, self.me, (self.ss, self.rs), self.dev = buf, me, sems, dev

        def one(self, n, slot, dev):
            return copy(self.buf.at[slot], self.buf.at[slot], self.ss.at[n], self.rs.at[slot], dev)

        def start(self):
            for n in FAR_FIRST:
                self.one(n, self.me, self.dev(wrap(self.me + n))).start()
            under_way.append(self)

        def arrived(self, n):
            slot = wrap(self.me + n)
            self.one(n, slot, self.dev(slot)).wait_recv()

        def wait(self):
            for n in NEAR_FIRST:
                self.arrived(n)
            self.wait = lambda: None

        def sent(self):
            for n in range(1, N):
                self.one(n, self.me, self.dev(wrap(self.me + n))).wait_send()

    class ChipGather(Gather):
        def start(self):
            for n in (4, 2, 6):
                self.one(n, g, on_g(wrap(g + n))).start()
            self.one(1, g, on_g(sib)).start()
            under_way.append(self)

        def wait(self):
            for n in (2, 6, 4):
                slot = wrap(g + n)
                self.one(n, slot, on_g(slot)).wait_recv()
                self.one(n + 1, slot, on_g(sib)).start()
            for n in (0, 2, 6, 4):
                slot = wrap(sib + n)
                self.one(1, slot, on_g(sib)).wait_recv()
            self.wait = lambda: None

        def sent(self):
            for n in range(1, N):
                self.one(n, g, on_g(sib)).wait_send()

    class Exchange(Gather):
        def __init__(self, src, buf, me, sems, dev):
            super().__init__(buf, me, sems, dev)
            self.src = src

        def to(self, n):
            i = wrap(self.me + n)
            return copy(self.src.at[i], self.buf.at[self.me], self.ss.at[n], self.rs.at[self.me], self.dev(i))

        def start(self):
            for n in FAR_FIRST:
                self.to(n).start()
            pltpu.make_async_copy(self.src.at[self.me], self.buf.at[self.me], self.rs.at[self.me]).start()
            under_way.append(self)

        def wait(self):
            for n in (0,) + NEAR_FIRST:
                self.arrived(n)
            self.wait = lambda: None

        def sent(self):
            for n in range(1, N):
                self.to(n).wait_send()

    class RelayGather(Gather):
        def __init__(self, src, buf, sems):
            super().__init__(buf, y, sems, on_y)
            self.src = src

        def own(self, n):
            return copy(self.src, self.buf.at[y], self.ss.at[n], self.rs.at[y], on_y(wrap(y + n)))

        def start(self):
            for n in (2, 6, 1, 7):
                self.own(n).start()
            under_way.append(self)

        def on(self, m):
            sign = 1 - 2 * lax.rem(y, 2)
            source, target = ((6, 1), (2, 7), (8 - 2 * sign, 8 + 2 * sign))[m]
            slot = wrap(y + source)
            return copy(
                self.buf.at[slot], self.buf.at[slot], self.ss.at[3 + m], self.rs.at[slot], on_y(wrap(y + target))
            )

        def relay(self):
            for n in (2, 6):
                self.arrived(n)
            for m in (2, 0, 1):
                self.on(m).start()
            self.relay = lambda: None

        def arrived(self, n):
            slot = wrap(y + n)
            self.one(0, slot, on_y(slot)).wait_recv()

        def wait(self):
            self.relay()
            for n in (1, 7, 3, 5, 4):
                self.arrived(n)
            self.wait = lambda: None

        def sent(self):
            for n in (2, 6, 1, 7):
                self.own(n).wait_send()
            for m in (0, 1, 2):
                self.on(m).wait_send()

    class Single:
        def __init__(self, src, dst, ss, rs, dev, own=None, recv=True):
            self.src, self.dst, self.rs, self.own, self.recv = src, dst, rs, own, recv
            self.away = copy(src, dst, ss, rs, dev)

        def apart(self, go):
            if self.own is None:
                go()
            else:
                pl.when(jnp.logical_not(self.own))(go)

        def start(self):
            self.apart(lambda: self.away.start())
            if self.own is not None:

                @pl.when(self.own)
                def _():
                    pltpu.make_async_copy(self.src, self.dst, self.rs).start()

            under_way.append(self)

        def wait(self):
            if self.recv:
                self.away.wait_recv()
            self.recv = False

        def sent(self):
            self.apart(lambda: self.away.wait_send())

    def drain():
        for item in under_way:
            item.wait()
        for item in under_way:
            item.sent()

    loads = {}
    for n, (name, src, dst) in enumerate(
        [
            ("vw", vw_in, vw), ("gain", gain_in, gain), ("q", q_in, q), ("k", k_in, k), ("wo", wo_in, wo), ("cot", cot_in, cot),
            ("x1", x_in.at[1], xt.at[1, y]), ("x0", x_in.at[0], xt.at[0, y]),
        ]
    ):
        loads[name] = pltpu.make_async_copy(src, dst, in_r.at[n])
        loads[name].start()

    barrier = pltpu.get_barrier_semaphore()

    def hello(dev):
        pl.semaphore_signal(barrier, inc=1, device_id=dev, device_id_type=MESH)

    for n in FAR_FIRST:
        hello(on_y(wrap(y + n)))
        hello(on_z(wrap(z + n)))
        hello(on_g(wrap(g + n)))

    shifts = tuple(c // 2 if c % 2 == 0 else (4 if c == 1 else 8 - c // 2) for c in range(N))
    shift = jnp.where(core == 0, g // 2, jnp.where(g == 1, 4, 8 - g // 2))
    head_here = shift == 0
    taker = on_y(wrap(y + 8 - shift))
    mirror = 7 - z
    rows32 = pl.multiple_of(32 * g, 32)
    mine = pl.ds(pl.multiple_of(HALF * near, 128), HALF)
    other = pl.ds(pl.multiple_of(HALF * (1 - near), 128), HALF)
    wo_chunk = [
        Single(wo_in.at[l, pl.ds(rows32, 32), :], wot.at[l, g], wz_s.at[l], wz_r.at[l], on_z(mirror)) for l in (0, 1)
    ]
    slice_rows = pl.ds(pl.multiple_of(32 * lax.rem(z, 4), 32), 32)
    swap_slice = Single(gvt.at[slice_rows, :], mrx, sw_s.at[0], sw_r.at[0], taker, head_here)
    taken = pl.ds(pl.multiple_of(FB * wrap(y + 8 - shift), 16), FB)
    swap_block = Single(vw_in.at[:, taken, :], vb.at[g], sw_s.at[1], sw_r.at[1], taker, head_here)
    inputs = [RelayGather(x_in.at[l], xt.at[l], (xt_s.at[l], xt_r.at[l])) for l in (0, 1)]
    products = Gather(mz, z, (mz_s, mz_r), on_z)
    maps = ChipGather(mt, g, (mt_s, mt_r), on_g)
    blocks = ChipGather(vb, g, (vb_s, vb_r), on_g)
    normed = [Exchange(xnp.at[l], xna.at[l], g, (xn_s.at[l], xn_r.at[l]), on_g) for l in (0, 1)]
    wo_parts = [ChipGather(wot.at[l], g, (wx_s.at[l], wx_r.at[l]), on_g) for l in (0, 1)]
    heads = [Gather(dvy.at[l], y, (dvy_s.at[l], dvy_r.at[l]), on_y) for l in (0, 1)]
    group = [Gather(dva.at[l], g, (dva_s.at[l], dva_r.at[l]), on_g) for l in (0, 1)]
    means = [Gather(mm.at[l], y, (mm_s.at[l], mm_r.at[l]), on_y) for l in (0, 1)]
    weights = [Exchange(dws.at[l], dwr.at[l], z, (dw_s.at[l], dw_r.at[l]), on_z) for l in (0, 1)]
    gains_y = Exchange(gys, gy, y, (gy_s, gy_r), on_y)
    gains_g = Gather(gx, g, (gx_s, gx_r), on_g)
    gains_z = Gather(gz, z, (gz_s, gz_r), on_z)

    pl.semaphore_wait(barrier, 3 * (N - 1))

    wo_chunk[1].start()
    inputs[1].start()

    loads["gain"].wait()
    loads["vw"].wait()
    for i in range(HALF // 128):
        rows = pl.ds(pl.multiple_of(HALF * near + 128 * i, 128), 128)
        part = jnp.transpose(vw[1, rows, :].astype(F32))
        gvt[:, 128 * i : 128 * i + 128] = (part * gain[1:2, rows]).astype(BF)
    swap_slice.start()
    wo_chunk[0].start()
    inputs[0].start()

    loads["q"].wait()
    loads["k"].wait()
    causal = lax.broadcasted_iota(jnp.int32, (TOK, TOK), 0) <= lax.broadcasted_iota(jnp.int32, (TOK, TOK), 1)
    for l in (1, 0):
        for h in (0, 1):
            scores = nt(k[l], q[l, :, HD * h : HD * h + HD])
            raised = jnp.where(causal, jnp.exp(50.0 * jnp.tanh(scores * (1.0 / 600.0))), 0.0)
            probs[2 * l + h] = (raised / jnp.sum(raised, axis=0, keepdims=True)).astype(BF)
    loads["wo"].wait()
    loads["cot"].wait()
    loads["x1"].wait()
    loads["x0"].wait()
    dctx1 = nt(wo[1], cot[:, mine])

    wo_chunk[1].wait()
    wo_parts[1].start()

    for i in range(D // 128):
        two = gain[:, 128 * i : 128 * i + 128]
        gcol[128 * i : 128 * i + 128, :] = jnp.transpose(jnp.concatenate([two, two, two, two], 0))
    swap_slice.wait()
    mz[z] = nt(mrx[...], wo[0]).astype(BF)
    products.start()
    wo_chunk[0].wait()
    wo_parts[0].start()

    inputs[1].relay()
    inputs[0].relay()

    wo_parts[1].wait()

    def values(l, dctx):
        return nt(probs[2 * l], dctx[0:HD]) + nt(probs[2 * l + 1], dctx[HD : 2 * HD])

    dctx1 = (dctx1 + nt(wot[1].reshape(2 * HD, HALF), cot[:, other])).astype(BF)
    dv = values(1, dctx1).astype(BF)
    dvy[1, y] = dv
    dva[1, g] = dv
    heads[1].start()
    group[1].start()

    def norm(l):
        total = jnp.zeros((1, TOK), F32)
        for b in range(N):
            xf = xt[l, b].astype(F32)
            total = total + jnp.sum(xf * xf, axis=0, keepdims=True)
        inv = lax.rsqrt(total * (1.0 / D) + 1e-6)
        inv_row[l : l + 1, :] = inv
        for b in range(N):
            xnb[l, b] = (xt[l, b].astype(F32) * inv * gcol[FB * b : FB * b + FB, l : l + 1]).astype(BF)

    def pack(l):
        for b in range(N):
            dwf[...] = xnb[l, b].astype(F32)
            for n in range(N):
                xnf[n, ROWS * b : ROWS * b + ROWS, :] = dwf[ROWS * n : ROWS * n + ROWS, :]
        for n in range(N):
            xnp[l, n] = xnf[n].astype(BF)
        normed[l].start()

    ones = jnp.ones((8, TOK), F32)

    def own_part(l):
        total = jnp.zeros((1, TOK), F32)
        for b in range(N):
            dxn = nt(vw[l, FB * b : FB * b + FB, :], dvy[l, y])
            prod = dxn * xnb[l, b].astype(F32)
            total = total + jnp.sum(prod, axis=0, keepdims=True)
            row = lax.dot_general(
                ones, prod, (((1,), (1,)), ((), ())), precision=lax.Precision.HIGHEST, preferred_element_type=F32
            )
            gys[b, l : l + 1, 0:FB] = row[0:1]
        mm[l, y] = jnp.broadcast_to(total * (1.0 / D), (8, TOK))
        means[l].start()

    products.wait()
    m_sum = mz[0:4].reshape(HD, 2 * HD).astype(F32) + mz[4:8].reshape(HD, 2 * HD).astype(F32)
    mt[g] = jnp.transpose(m_sum).astype(BF)
    maps.start()

    inputs[1].wait()
    gys[...] = jnp.zeros((N, 8, 384), F32)
    norm(1)
    own_part(1)
    swap_block.start()

    inputs[0].wait()
    norm(0)
    pack(0)

    wo_parts[0].wait()
    wo_other = wot[0].reshape(2 * HD, HALF)
    base = nt(wo[0], cot[:, mine]) + nt(wo_other, cot[:, other])
    xt_half = [xt[1, 0:4].reshape(HALF, TOK), xt[1, 4:8].reshape(HALF, TOK)]
    first = near == 0
    xt_mine = jnp.where(first, xt_half[0], xt_half[1])
    xt_other = jnp.where(first, xt_half[1], xt_half[0])
    y1 = nn(wo[0], xt_mine) + nn(wo_other, xt_other)
    pack(1)
    swap_block.wait()
    blocks.start()

    maps.wait()
    heads[1].wait()

    def over_heads(left, l):
        total = nt(left(0), dvy[l, wrap(y + shifts[0])])
        for n in range(1, N):
            total = total + nt(left(n), dvy[l, wrap(y + shifts[n])])
        return total

    corr = over_heads(lambda n: mt[n], 1)
    means[1].wait()
    inv1 = inv_row[1:2, :]
    mean1 = sum_of(mm.at[1])[0:1, :]
    dctx0 = (base + inv1 * (corr - (inv1 * mean1) * y1)).astype(BF)
    dv = values(0, dctx0).astype(BF)
    dvy[0, y] = dv
    dva[0, g] = dv
    group[0].start()
    heads[0].start()
    own_part(0)
    gains_y.start()

    def weight_grad(l):
        block = nn(xna[l, 0], dva[l, 0])
        for n in range(1, N):
            block = block + nn(xna[l, n], dva[l, n])
        dwf[...] = block * scale
        for n in range(N):
            dws[l, n, 0:ROWS, :] = dwf[ROWS * n : ROWS * n + ROWS, :]
            dws[l, n, ROWS:40, :] = jnp.zeros((40 - ROWS, HD), F32)
        weights[l].start()

    def weight_sum(l):
        weights[l].wait()
        dw_out[:, l, :] = sum_of(dwr.at[l])[0:ROWS]

    own_rows = pl.ds(pl.multiple_of(FB * y, 32), FB)

    def input_grad(l, mean):
        dxn = over_heads(lambda n: vb[n, l], l)
        inv = inv_row[l : l + 1, :]
        return inv * (dxn * gcol[own_rows, l : l + 1] - xt[l, y].astype(F32) * (inv * mean))

    normed[1].wait()
    group[1].wait()
    weight_grad(1)
    normed[0].wait()
    group[0].wait()
    weight_grad(0)

    gains_y.wait()
    gx[g] = sum_of(gy)
    gains_g.start()

    for b in range(N):

        @pl.when(y == b)
        def _():
            pad[:, 0:FB] = cot[:, FB * b : FB * b + FB].astype(F32)
            gain_blk[...] = gain[:, FB * b : FB * b + FB]

    cot_blk[0:128, :] = jnp.transpose(pad[:, 0:128])
    cot_blk[128:256, :] = jnp.transpose(pad[:, 128:256])
    cot_blk[256:288, :] = jnp.transpose(pad[:, 256:384])[0:32]
    blocks.wait()
    cot1 = (cot_blk[...] + input_grad(1, mean1)).astype(BF).astype(F32)

    gains_g.wait()
    gz[z] = sum_of(gx)
    gains_z.start()

    heads[0].wait()
    means[0].wait()
    out[...] = (cot1 + input_grad(0, sum_of(mm.at[0])[0:1, :])).astype(BF)

    weight_sum(1)
    weight_sum(0)
    gains_z.wait()
    gain_out[...] = sum_of(gz)[0:2, 0:FB] * scale / gain_blk[...]
    drain()


def body(grad_output, layer_input, norm_gain, queries, keys, value_weight, output_weight):
    vmem = pltpu.VMEM
    dma = pltpu.SemaphoreType.DMA
    one = [dma((N,)), dma((N,))]
    two = [dma((2, N)), dma((2, N))]
    pair = [dma((2,)), dma((2,))]
    hbm = pl.BlockSpec(memory_space=pltpu.HBM)
    out, weights, gains = pl.pallas_call(
        kernel,
        out_shape=(
            jax.ShapeDtypeStruct((FB, TOK), BF),
            jax.ShapeDtypeStruct((ROWS, 2, HD), F32),
            jax.ShapeDtypeStruct((2, FB), F32),
        ),
        in_specs=[hbm] * 7,
        out_specs=[pl.BlockSpec(memory_space=vmem)] * 3,
        scratch_shapes=[
            vmem((TOK, D), BF),
            vmem((2, D), F32),
            vmem((2, TOK, 2 * HD), BF),
            vmem((2, TOK, HD), BF),
            vmem((2, D, HD), BF),
            vmem((2, 2 * HD, HALF), BF),
            vmem((2, N, FB, TOK), BF),
            vmem((D, 8), F32),
            vmem((HD, HALF), BF),
            vmem((4, TOK, TOK), BF),
            vmem((2, N, 32, HALF), BF),
            vmem((32, HALF), BF),
            vmem((N, 32, 2 * HD), BF),
            vmem((N, 2 * HD, HD), BF),
            vmem((N, 2, FB, HD), BF),
            vmem((2, N, FB, TOK), BF),
            vmem((N, FB, TOK), F32),
            vmem((2, N, FB, TOK), BF),
            vmem((2, N, FB, TOK), BF),
            vmem((2, N, TOK, HD), BF),
            vmem((2, N, TOK, HD), BF),
            vmem((2, N, 8, TOK), F32),
            vmem((N, 8, 384), F32),
            vmem((N, 8, 384), F32),
            vmem((N, 8, 384), F32),
            vmem((N, 8, 384), F32),
            vmem((FB, HD), F32),
            vmem((2, N, 40, HD), F32),
            vmem((2, N, 40, HD), F32),
            vmem((TOK, 384), F32),
            vmem((FB, TOK), F32),
            vmem((2, FB), F32),
            vmem((8, TOK), F32),
        ]
        + [dma((8,))]
        + two
        + pair
        + pair
        + two
        + one
        + one
        + one
        + two
        + two
        + two
        + two
        + one
        + one
        + one
        + two,
        compiler_params=pltpu.CompilerParams(
            collective_id=0, has_side_effects=True, vmem_limit_bytes=63 * 2**20
        ),
    )(grad_output, jnp.swapaxes(layer_input, 1, 2), norm_gain, queries, keys, value_weight, output_weight)
    return jnp.swapaxes(out, 0, 1), jnp.swapaxes(weights, 0, 1), gains


def solution(mesh):
    return jax.shard_map(
        body,
        mesh=mesh,
        in_specs=(
            P(("near", "far"), None),
            P(None, ("near", "far"), "tensor"),
            P(),
            P(None, ("near", "far"), "tensor"),
            P(None, ("near", "far"), "tensor"),
            P(None, None, "tensor"),
            P(None, "tensor", "near"),
        ),
        out_specs=(
            P(("near", "far"), "tensor"),
            P(None, ("near", "far"), "tensor"),
            P(None, "tensor"),
        ),
        check_vma=False,
    )
```

time: 524 us -> 79 us (0.15)
  waiting for transfers between devices: 346 us -> 0 us
  blocking collectives: 131 us -> 0 us
  Pallas kernels: 0 us -> 74 us
  between operations: 15 us -> 0.64 us
  local copies, waits for them, and re-layouts: 15.5 us -> 4.17 us
  matrix products: 10.3 us -> 0 us
    psum x2 -> x0, waiting for transfers between devices: 139 us -> none  [body(): lax.psum(partial_term.astype(jnp.bfloat16), 'tensor').astype(jnp.float32)]
    all_gather x3 -> x0, waiting for transfers between devices: 134 us -> none  [the longest x2 104 us: body(): lax.all_gather(output_weight[depth_index], 'near', axis=1, tiled=True)]
    psum x1 -> x0, blocking collectives: 131 us -> none  [body(): gain_stack = lax.psum(jnp.stack(gain_grads), ('near', 'far'))]
    unnamed x7 -> x0, waiting for transfers between devices: 74.4 us -> none
    pallas_call x0 -> x1, Pallas kernels: none -> 74 us  [body(): pl.pallas_call(kernel, out_shape=(jax.ShapeDtypeStruct((FB, TOK), BF), ja...]
    dot_general x10 -> x0, matrix products: 10.3 us -> none  [the longest x2 3.72 us: body(): lax.dot_general(current, lax.all_gather(output_weight[depth_index], 'near...]
    slice x6 -> x0, local copies, waits for them, and re-layouts: 6.84 us -> none  [the longest x1 3.75 us: body(): rows_full = inputs[depth_index].astype(jnp.float32)]
  transfers between devices with their start and end apart: 6 -> 0, of which waited for: 6 -> 0; matrix products, arithmetic and copies ran while one was open for 4% -> 0% of each run, Pallas kernels for 0% -> 0%
where the time goes in v2:
time: 79 us; the launch traced here: 78.8 us
  Pallas kernels  74 us (94%)
  local copies, waits for them, and re-layouts  4.17 us (5%)
    pallas_call x1, Pallas kernels, body(): pl.pallas_call(kernel, out_shape=(jax.ShapeDtypeStruct((FB, TOK), BF), ja...  74 us
    unnamed x3, local copies, waits for them, and re-layouts  4.17 us

profile of v2, /device:TPU:1, one launch (start us, length us, event | category | flops | bytes accessed | tf_op | source)
XLA Modules:
  0.0 78.8 jit_solution(5100097887933901097)
XLA Ops:
  0.6 74.0 %shard_map.94 = (bf16[288,128]{1,0:T(8,128)(2,1)}, f32[36,2,128]{2,1,0:T(2,128)}, f32[2,288]{1,0:T(2,128)}) custom-call(bf16[128,2304]{1,0:T(8,128)(2,1)} %cot_in.1, bf16[2,288,128]{2,1,0:T(8,128)(2,1)} %bitcast.3, f32[2,2304]{1,0:T(2,128)} %gain_in.1, bf16[2,128,256]{2,1,0:T(8,128)(2,1)} %q_in.1, bf16[2,128,128]{2,1,0:T(8,128)(2,1)} %k_in.1, ...), custom_call_target="tpu_custom_call" | custom-call | tf_op jit(solution)/shard_map/pallas_call | solution.py:485
  74.6 1.5 %copy.13 = bf16[128,288]{0,1:T(8,128)(2,1)} copy(bf16[128,288]{0,1:T(8,128)(2,1)} %bitcast.4) | data formatting | bytes 147456
  76.1 1.4 %copy.14 = f32[2,36,128]{2,0,1:T(2,128)} copy(f32[2,36,128]{2,0,1:T(2,128)} %bitcast.5) | data formatting | bytes 73728
  77.5 1.3 %copy.15 = f32[2,288]{1,0:T(2,128)} copy(f32[2,288]{1,0:T(2,128)} %get-tuple-element.14) | data formatting | bytes 4608

commit v3 on v2

--- a/solution.py
+++ b/solution.py
@@ -48,10 +48,10 @@
 def kernel(
     cot_in, x_in, gain_in, q_in, k_in, vw_in, wo_in,
     out, dw_out, gain_out,
-    cot, gain, q, k, vw, wo,
-    xt, gcol, gvt, probs, wot, mrx, mz, mt, vb, xnb, xnf, xnp, xna, dvy, dva, mm, gys, gy, gx, gz, dwf, dws, dwr, pad, cot_blk, gain_blk, inv_row,
-    in_r, xt_s, xt_r, sw_s, sw_r, wz_s, wz_r, wx_s, wx_r, mz_s, mz_r, mt_s, mt_r, vb_s, vb_r, xn_s, xn_r,
-    dvy_s, dvy_r, dva_s, dva_r, mm_s, mm_r, gy_s, gy_r, gx_s, gx_r, gz_s, gz_r, dw_s, dw_r,
+    cot, gain, q, k, vw, wo, x0,
+    xt, x0p, x0a, x0y, x0w, gcol, gvt, probs, wot, mrx, mz, mt, vb, xnb, xnf, xnp, xna, dvy, dva, sq, mm, gx, gz, dwf, dws, dwr, pad, cot_blk,
+    in_r, xt_s, xt_r, x0a_s, x0a_r, x0y_s, x0y_r, sw_s, sw_r, wz_s, wz_r, wx_s, wx_r, mz_s, mz_r, mt_s, mt_r, vb_s, vb_r, xn_s, xn_r,
+    dvy_s, dvy_r, dva_s, dva_r, sq_s, sq_r, mm_s, mm_r, gx_s, gx_r, gz_s, gz_r, dw_s, dw_r,
 ):
     scale = 1.0 / math.sqrt(8192.0)
     y = lax.axis_index("tensor")
@@ -110,11 +110,15 @@
             self.one(1, g, on_g(sib)).start()
             under_way.append(self)
 
-        def wait(self):
+        def pass_on(self):
             for n in (2, 6, 4):
                 slot = wrap(g + n)
                 self.one(n, slot, on_g(slot)).wait_recv()
                 self.one(n + 1, slot, on_g(sib)).start()
+            self.pass_on = lambda: None
+
+        def wait(self):
+            self.pass_on()
             for n in (0, 2, 6, 4):
                 slot = wrap(sib + n)
                 self.one(1, slot, on_g(sib)).wait_recv()
@@ -230,8 +234,8 @@
     loads = {}
     for n, (name, src, dst) in enumerate(
         [
-            ("vw", vw_in, vw), ("gain", gain_in, gain), ("q", q_in, q), ("k", k_in, k), ("wo", wo_in, wo), ("cot", cot_in, cot),
-            ("x1", x_in.at[1], xt.at[1, y]), ("x0", x_in.at[0], xt.at[0, y]),
+            ("x0", x_in.at[0], x0), ("gain", gain_in, gain), ("vw", vw_in, vw), ("q", q_in, q), ("k", k_in, k),
+            ("wo", wo_in, wo), ("cot", cot_in, cot), ("x1", x_in.at[1], xt.at[y]),
         ]
     ):
         loads[name] = pltpu.make_async_copy(src, dst, in_r.at[n])
@@ -262,24 +266,30 @@
     swap_slice = Single(gvt.at[slice_rows, :], mrx, sw_s.at[0], sw_r.at[0], taker, head_here)
     taken = pl.ds(pl.multiple_of(FB * wrap(y + 8 - shift), 16), FB)
     swap_block = Single(vw_in.at[:, taken, :], vb.at[g], sw_s.at[1], sw_r.at[1], taker, head_here)
-    inputs = [RelayGather(x_in.at[l], xt.at[l], (xt_s.at[l], xt_r.at[l])) for l in (0, 1)]
+    inputs = RelayGather(x_in.at[1], xt, (xt_s, xt_r))
+    squares = Gather(sq, y, (sq_s, sq_r), on_y)
+    mixed = Exchange(x0p, x0a, g, (x0a_s, x0a_r), on_g)
+    mixed_y = RelayGather(x0y.at[y], x0y, (x0y_s, x0y_r))
     products = Gather(mz, z, (mz_s, mz_r), on_z)
     maps = ChipGather(mt, g, (mt_s, mt_r), on_g)
     blocks = ChipGather(vb, g, (vb_s, vb_r), on_g)
-    normed = [Exchange(xnp.at[l], xna.at[l], g, (xn_s.at[l], xn_r.at[l]), on_g) for l in (0, 1)]
+    normed = Exchange(xnp, xna, g, (xn_s, xn_r), on_g)
     wo_parts = [ChipGather(wot.at[l], g, (wx_s.at[l], wx_r.at[l]), on_g) for l in (0, 1)]
     heads = [Gather(dvy.at[l], y, (dvy_s.at[l], dvy_r.at[l]), on_y) for l in (0, 1)]
     group = [Gather(dva.at[l], g, (dva_s.at[l], dva_r.at[l]), on_g) for l in (0, 1)]
     means = [Gather(mm.at[l], y, (mm_s.at[l], mm_r.at[l]), on_y) for l in (0, 1)]
     weights = [Exchange(dws.at[l], dwr.at[l], z, (dw_s.at[l], dw_r.at[l]), on_z) for l in (0, 1)]
-    gains_y = Exchange(gys, gy, y, (gy_s, gy_r), on_y)
     gains_g = Gather(gx, g, (gx_s, gx_r), on_g)
     gains_z = Gather(gz, z, (gz_s, gz_r), on_z)
 
     pl.semaphore_wait(barrier, 3 * (N - 1))
 
     wo_chunk[1].start()
-    inputs[1].start()
+    inputs.start()
+    loads["x0"].wait()
+    xf = x0[...].astype(F32)
+    sq[y] = jnp.broadcast_to(jnp.sum(xf * xf, axis=0, keepdims=True), (8, TOK))
+    squares.start()
 
     loads["gain"].wait()
     loads["vw"].wait()
@@ -289,37 +299,46 @@
         gvt[:, 128 * i : 128 * i + 128] = (part * gain[1:2, rows]).astype(BF)
     swap_slice.start()
     wo_chunk[0].start()
-    inputs[0].start()
+    swap_block.start()
 
     loads["q"].wait()
     loads["k"].wait()
     causal = lax.broadcasted_iota(jnp.int32, (TOK, TOK), 0) <= lax.broadcasted_iota(jnp.int32, (TOK, TOK), 1)
-    for l in (1, 0):
+
+    def attend(l):
         for h in (0, 1):
             scores = nt(k[l], q[l, :, HD * h : HD * h + HD])
             raised = jnp.where(causal, jnp.exp(50.0 * jnp.tanh(scores * (1.0 / 600.0))), 0.0)
             probs[2 * l + h] = (raised / jnp.sum(raised, axis=0, keepdims=True)).astype(BF)
+
+    attend(1)
     loads["wo"].wait()
     loads["cot"].wait()
     loads["x1"].wait()
-    loads["x0"].wait()
     dctx1 = nt(wo[1], cot[:, mine])
 
     wo_chunk[1].wait()
     wo_parts[1].start()
+    swap_slice.wait()
+    mz[z] = nt(mrx[...], wo[0]).astype(BF)
+    products.start()
 
     for i in range(D // 128):
         two = gain[:, 128 * i : 128 * i + 128]
         gcol[128 * i : 128 * i + 128, :] = jnp.transpose(jnp.concatenate([two, two, two, two], 0))
-    swap_slice.wait()
-    mz[z] = nt(mrx[...], wo[0]).astype(BF)
-    products.start()
+    own_rows = pl.ds(pl.multiple_of(FB * y, 32), FB)
+
+    squares.wait()
+    inv0 = lax.rsqrt(sum_of(sq)[0:1] * (1.0 / D) + 1e-6)
+    dwf[...] = x0[...].astype(F32) * inv0 * gcol[own_rows, 0:1]
+    for n in range(N):
+        x0p[n] = jnp.concatenate([dwf[ROWS * n : ROWS * n + ROWS, :], jnp.zeros((48 - ROWS, TOK), F32)], 0).astype(BF)
+    mixed.start()
+
     wo_chunk[0].wait()
     wo_parts[0].start()
 
-    inputs[1].relay()
-    inputs[0].relay()
-
+    inputs.relay()
     wo_parts[1].wait()
 
     def values(l, dctx):
@@ -331,67 +350,57 @@
     dva[1, g] = dv
     heads[1].start()
     group[1].start()
-
-    def norm(l):
-        total = jnp.zeros((1, TOK), F32)
+    attend(0)
+
+    def regroup(part):
         for b in range(N):
-            xf = xt[l, b].astype(F32)
-            total = total + jnp.sum(xf * xf, axis=0, keepdims=True)
-        inv = lax.rsqrt(total * (1.0 / D) + 1e-6)
-        inv_row[l : l + 1, :] = inv
-        for b in range(N):
-            xnb[l, b] = (xt[l, b].astype(F32) * inv * gcol[FB * b : FB * b + FB, l : l + 1]).astype(BF)
-
-    def pack(l):
-        for b in range(N):
-            dwf[...] = xnb[l, b].astype(F32)
+            dwf[...] = part(b).astype(F32)
             for n in range(N):
                 xnf[n, ROWS * b : ROWS * b + ROWS, :] = dwf[ROWS * n : ROWS * n + ROWS, :]
-        for n in range(N):
-            xnp[l, n] = xnf[n].astype(BF)
-        normed[l].start()
-
-    ones = jnp.ones((8, TOK), F32)
-
-    def own_part(l):
-        total = jnp.zeros((1, TOK), F32)
-        for b in range(N):
-            dxn = nt(vw[l, FB * b : FB * b + FB, :], dvy[l, y])
-            prod = dxn * xnb[l, b].astype(F32)
-            total = total + jnp.sum(prod, axis=0, keepdims=True)
-            row = lax.dot_general(
-                ones, prod, (((1,), (1,)), ((), ())), precision=lax.Precision.HIGHEST, preferred_element_type=F32
-            )
-            gys[b, l : l + 1, 0:FB] = row[0:1]
-        mm[l, y] = jnp.broadcast_to(total * (1.0 / D), (8, TOK))
-        means[l].start()
 
     products.wait()
     m_sum = mz[0:4].reshape(HD, 2 * HD).astype(F32) + mz[4:8].reshape(HD, 2 * HD).astype(F32)
     mt[g] = jnp.transpose(m_sum).astype(BF)
     maps.start()
 
-    inputs[1].wait()
-    gys[...] = jnp.zeros((N, 8, 384), F32)
-    norm(1)
-    own_part(1)
-    swap_block.start()
-
-    inputs[0].wait()
-    norm(0)
-    pack(0)
-
+    mixed.wait()
+    for n in range(N):
+        dwf[ROWS * n : ROWS * n + ROWS, :] = x0a[n].astype(F32)[0:ROWS]
+    x0y[y] = dwf[...].astype(BF)
+    mixed_y.start()
+
+    swap_block.wait()
+    blocks.start()
+    wo_parts[0].pass_on()
+
+    inputs.wait()
+    total = jnp.zeros((1, TOK), F32)
+    for b in range(N):
+        xf = xt[b].astype(F32)
+        total = total + jnp.sum(xf * xf, axis=0, keepdims=True)
+    inv1 = lax.rsqrt(total * (1.0 / D) + 1e-6)
+    total = jnp.zeros((1, TOK), F32)
+    for b in range(N):
+        xnb[b] = (xt[b].astype(F32) * inv1 * gcol[FB * b : FB * b + FB, 1:2]).astype(BF)
+        dxn = nt(vw[1, FB * b : FB * b + FB, :], dvy[1, y])
+        total = total + jnp.sum(dxn * xnb[b].astype(F32), axis=0, keepdims=True)
+    mm[1, y] = jnp.broadcast_to(total * (1.0 / D), (8, TOK))
+    means[1].start()
+
+    maps.pass_on()
     wo_parts[0].wait()
     wo_other = wot[0].reshape(2 * HD, HALF)
     base = nt(wo[0], cot[:, mine]) + nt(wo_other, cot[:, other])
-    xt_half = [xt[1, 0:4].reshape(HALF, TOK), xt[1, 4:8].reshape(HALF, TOK)]
+    xt_half = [xt[0:4].reshape(HALF, TOK), xt[4:8].reshape(HALF, TOK)]
     first = near == 0
     xt_mine = jnp.where(first, xt_half[0], xt_half[1])
     xt_other = jnp.where(first, xt_half[1], xt_half[0])
     y1 = nn(wo[0], xt_mine) + nn(wo_other, xt_other)
-    pack(1)
-    swap_block.wait()
-    blocks.start()
+    regroup(lambda b: xnb[b])
+    for n in range(N):
+        xnp[n] = xnf[n].astype(BF)
+    normed.start()
+    mixed_y.relay()
 
     maps.wait()
     heads[1].wait()
@@ -404,7 +413,6 @@
 
     corr = over_heads(lambda n: mt[n], 1)
     means[1].wait()
-    inv1 = inv_row[1:2, :]
     mean1 = sum_of(mm.at[1])[0:1, :]
     dctx0 = (base + inv1 * (corr - (inv1 * mean1) * y1)).astype(BF)
     dv = values(0, dctx0).astype(BF)
@@ -412,13 +420,22 @@
     dva[0, g] = dv
     group[0].start()
     heads[0].start()
-    own_part(0)
-    gains_y.start()
-
-    def weight_grad(l):
-        block = nn(xna[l, 0], dva[l, 0])
+    blocks.pass_on()
+
+    for b in range(N):
+
+        @pl.when(y == b)
+        def _():
+            pad[:, 0:FB] = cot[:, FB * b : FB * b + FB].astype(F32)
+
+    cot_blk[0:128, :] = jnp.transpose(pad[:, 0:128])
+    cot_blk[128:256, :] = jnp.transpose(pad[:, 128:256])
+    cot_blk[256:288, :] = jnp.transpose(pad[:, 256:384])[0:32]
+
+    def weight_grad(l, left):
+        block = nn(left(0), dva[l, 0])
         for n in range(1, N):
-            block = block + nn(xna[l, n], dva[l, n])
+            block = block + nn(left(n), dva[l, n])
         dwf[...] = block * scale
         for n in range(N):
             dws[l, n, 0:ROWS, :] = dwf[ROWS * n : ROWS * n + ROWS, :]
@@ -429,49 +446,48 @@
         weights[l].wait()
         dw_out[:, l, :] = sum_of(dwr.at[l])[0:ROWS]
 
-    own_rows = pl.ds(pl.multiple_of(FB * y, 32), FB)
-
-    def input_grad(l, mean):
+    ones = jnp.ones((8, TOK), F32)
+
+    def input_grad(l, own, inv):
         dxn = over_heads(lambda n: vb[n, l], l)
-        inv = inv_row[l : l + 1, :]
-        return inv * (dxn * gcol[own_rows, l : l + 1] - xt[l, y].astype(F32) * (inv * mean))
-
-    normed[1].wait()
+        xhat = own * inv
+        row = lax.dot_general(
+            ones, dxn * xhat, (((1,), (1,)), ((), ())), precision=lax.Precision.HIGHEST, preferred_element_type=F32
+        )
+        gx[g, l : l + 1, 0:FB] = row[0:1] * scale
+        return xhat, dxn * gcol[own_rows, l : l + 1]
+
+    normed.wait()
     group[1].wait()
-    weight_grad(1)
-    normed[0].wait()
+    weight_grad(1, lambda n: xna[n])
+    mixed_y.wait()
+    regroup(lambda b: x0y[b])
+    for n in range(N):
+        x0w[n] = xnf[n].astype(BF)
+    gx[g] = jnp.zeros((8, 384), F32)
+    blocks.wait()
+    xhat, gg = input_grad(1, xt[y].astype(F32), inv1)
+    cot_blk[...] = (cot_blk[...] + inv1 * (gg - xhat * mean1)).astype(BF).astype(F32)
+
     group[0].wait()
-    weight_grad(0)
-
-    gains_y.wait()
-    gx[g] = sum_of(gy)
+    weight_grad(0, lambda n: x0w[n])
+
+    heads[0].wait()
+    xhat, gg = input_grad(0, x0[...].astype(F32), inv0)
     gains_g.start()
-
-    for b in range(N):
-
-        @pl.when(y == b)
-        def _():
-            pad[:, 0:FB] = cot[:, FB * b : FB * b + FB].astype(F32)
-            gain_blk[...] = gain[:, FB * b : FB * b + FB]
-
-    cot_blk[0:128, :] = jnp.transpose(pad[:, 0:128])
-    cot_blk[128:256, :] = jnp.transpose(pad[:, 128:256])
-    cot_blk[256:288, :] = jnp.transpose(pad[:, 256:384])[0:32]
-    blocks.wait()
-    cot1 = (cot_blk[...] + input_grad(1, mean1)).astype(BF).astype(F32)
-
+    mm[0, y] = jnp.broadcast_to(jnp.sum(gg * xhat, axis=0, keepdims=True) * (1.0 / D), (8, TOK))
+    means[0].start()
     gains_g.wait()
     gz[z] = sum_of(gx)
     gains_z.start()
 
-    heads[0].wait()
     means[0].wait()
-    out[...] = (cot1 + input_grad(0, sum_of(mm.at[0])[0:1, :])).astype(BF)
+    out[...] = (cot_blk[...] + inv0 * (gg - xhat * sum_of(mm.at[0])[0:1, :])).astype(BF)
 
     weight_sum(1)
     weight_sum(0)
     gains_z.wait()
-    gain_out[...] = sum_of(gz)[0:2, 0:FB] * scale / gain_blk[...]
+    gain_out[...] = sum_of(gz)[0:2, 0:FB]
     drain()
 
 
@@ -498,7 +514,12 @@
             vmem((2, TOK, HD), BF),
             vmem((2, D, HD), BF),
             vmem((2, 2 * HD, HALF), BF),
-            vmem((2, N, FB, TOK), BF),
+            vmem((FB, TOK), BF),
+            vmem((N, FB, TOK), BF),
+            vmem((N, 48, TOK), BF),
+            vmem((N, 48, TOK), BF),
+            vmem((N, FB, TOK), BF),
+            vmem((N, FB, TOK), BF),
             vmem((D, 8), F32),
             vmem((HD, HALF), BF),
             vmem((4, TOK, TOK), BF),
@@ -507,15 +528,14 @@
             vmem((N, 32, 2 * HD), BF),
             vmem((N, 2 * HD, HD), BF),
             vmem((N, 2, FB, HD), BF),
-            vmem((2, N, FB, TOK), BF),
+            vmem((N, FB, TOK), BF),
             vmem((N, FB, TOK), F32),
-            vmem((2, N, FB, TOK), BF),
-            vmem((2, N, FB, TOK), BF),
+            vmem((N, FB, TOK), BF),
+            vmem((N, FB, TOK), BF),
             vmem((2, N, TOK, HD), BF),
             vmem((2, N, TOK, HD), BF),
+            vmem((N, 8, TOK), F32),
             vmem((2, N, 8, TOK), F32),
-            vmem((N, 8, 384), F32),
-            vmem((N, 8, 384), F32),
             vmem((N, 8, 384), F32),
             vmem((N, 8, 384), F32),
             vmem((FB, HD), F32),
@@ -523,22 +543,22 @@
             vmem((2, N, 40, HD), F32),
             vmem((TOK, 384), F32),
             vmem((FB, TOK), F32),
-            vmem((2, FB), F32),
-            vmem((8, TOK), F32),
         ]
         + [dma((8,))]
-        + two
+        + one
+        + one
+        + one
         + pair
         + pair
         + two
         + one
         + one
         + one
+        + one
         + two
         + two
+        + one
         + two
-        + two
-        + one
         + one
         + one
         + two,

time: 79 us -> 72.7 us (0.920)
  Pallas kernels: 74 us -> 67.6 us
    pallas_call x1, Pallas kernels: 74 us -> 67.6 us  [body(): pl.pallas_call(kernel, out_shape=(jax.ShapeDtypeStruct((FB, TOK), BF), ja...]
where the time goes in v3:
time: 72.7 us; the launch traced here: 72.4 us
  Pallas kernels  67.6 us (93%)
  local copies, waits for them, and re-layouts  4.17 us (6%)
    pallas_call x1, Pallas kernels, body(): pl.pallas_call(kernel, out_shape=(jax.ShapeDtypeStruct((FB, TOK), BF), ja...  67.6 us
    unnamed x3, local copies, waits for them, and re-layouts  4.17 us

profile of v3, /device:TPU:1, one launch (start us, length us, event | category | flops | bytes accessed | tf_op | source)
XLA Modules:
  0.0 72.4 jit_solution(16060654068378895758)
XLA Ops:
  0.6 67.6 %shard_map.94 = (bf16[288,128]{1,0:T(8,128)(2,1)}, f32[36,2,128]{2,1,0:T(2,128)}, f32[2,288]{1,0:T(2,128)}) custom-call(bf16[128,2304]{1,0:T(8,128)(2,1)} %cot_in.1, bf16[2,288,128]{2,1,0:T(8,128)(2,1)} %bitcast.3, f32[2,2304]{1,0:T(2,128)} %gain_in.1, bf16[2,128,256]{2,1,0:T(8,128)(2,1)} %q_in.1, bf16[2,128,128]{2,1,0:T(8,128)(2,1)} %k_in.1, ...), custom_call_target="tpu_custom_call" | custom-call | tf_op jit(solution)/shard_map/pallas_call | solution.py:501
  68.2 1.5 %copy.13 = bf16[128,288]{0,1:T(8,128)(2,1)} copy(bf16[128,288]{0,1:T(8,128)(2,1)} %bitcast.4) | data formatting | bytes 147456
  69.8 1.4 %copy.14 = f32[2,36,128]{2,0,1:T(2,128)} copy(f32[2,36,128]{2,0,1:T(2,128)} %bitcast.5) | data formatting | bytes 73728
  71.1 1.3 %copy.15 = f32[2,288]{1,0:T(2,128)} copy(f32[2,288]{1,0:T(2,128)} %get-tuple-element.14) | data formatting | bytes 4608

commit v4 on v3

--- a/solution.py
+++ b/solution.py
@@ -49,7 +49,7 @@
     cot_in, x_in, gain_in, q_in, k_in, vw_in, wo_in,
     out, dw_out, gain_out,
     cot, gain, q, k, vw, wo, x0,
-    xt, x0p, x0a, x0y, x0w, gcol, gvt, probs, wot, mrx, mz, mt, vb, xnb, xnf, xnp, xna, dvy, dva, sq, mm, gx, gz, dwf, dws, dwr, pad, cot_blk,
+    xt, x0p, x0a, x0y, x0w, gcol, gvt, probs, wot, mrx, mz, mt, vb, xnb, xnf, xna, dvy, dva, sq, mm, gx, gz, dwf, dws, dwr, pad, cot_blk,
     in_r, xt_s, xt_r, x0a_s, x0a_r, x0y_s, x0y_r, sw_s, sw_r, wz_s, wz_r, wx_s, wx_r, mz_s, mz_r, mt_s, mt_r, vb_s, vb_r, xn_s, xn_r,
     dvy_s, dvy_r, dva_s, dva_r, sq_s, sq_r, mm_s, mm_r, gx_s, gx_r, gz_s, gz_r, dw_s, dw_r,
 ):
@@ -234,8 +234,8 @@
     loads = {}
     for n, (name, src, dst) in enumerate(
         [
-            ("x0", x_in.at[0], x0), ("gain", gain_in, gain), ("vw", vw_in, vw), ("q", q_in, q), ("k", k_in, k),
-            ("wo", wo_in, wo), ("cot", cot_in, cot), ("x1", x_in.at[1], xt.at[y]),
+            ("x0", x_in.at[0], x0), ("gain", gain_in, gain), ("vw", vw_in.at[1], vw), ("q", q_in, q), ("k", k_in, k),
+            ("wo1", wo_in.at[1], wo.at[1]), ("cot", cot_in, cot), ("wo0", wo_in.at[0], wo.at[0]), ("x1", x_in.at[1], xt.at[y]),
         ]
     ):
         loads[name] = pltpu.make_async_copy(src, dst, in_r.at[n])
@@ -273,18 +273,26 @@
     products = Gather(mz, z, (mz_s, mz_r), on_z)
     maps = ChipGather(mt, g, (mt_s, mt_r), on_g)
     blocks = ChipGather(vb, g, (vb_s, vb_r), on_g)
-    normed = Exchange(xnp, xna, g, (xn_s, xn_r), on_g)
+    normed = Exchange(xnb, xna, z, (xn_s, xn_r), on_z)
     wo_parts = [ChipGather(wot.at[l], g, (wx_s.at[l], wx_r.at[l]), on_g) for l in (0, 1)]
-    heads = [Gather(dvy.at[l], y, (dvy_s.at[l], dvy_r.at[l]), on_y) for l in (0, 1)]
-    group = [Gather(dva.at[l], g, (dva_s.at[l], dva_r.at[l]), on_g) for l in (0, 1)]
+    heads = [
+        Gather(dvy.at[0], y, (dvy_s.at[0], dvy_r.at[0]), on_y),
+        RelayGather(dvy.at[1, y], dvy.at[1], (dvy_s.at[1], dvy_r.at[1])),
+    ]
+    group = [
+        Gather(dva.at[l], (g, z)[l], (dva_s.at[l], dva_r.at[l]), (on_g, on_z)[l]) for l in (0, 1)
+    ]
     means = [Gather(mm.at[l], y, (mm_s.at[l], mm_r.at[l]), on_y) for l in (0, 1)]
-    weights = [Exchange(dws.at[l], dwr.at[l], z, (dw_s.at[l], dw_r.at[l]), on_z) for l in (0, 1)]
+    weights = [
+        Exchange(dws.at[l], dwr.at[l], (z, g)[l], (dw_s.at[l], dw_r.at[l]), (on_z, on_g)[l]) for l in (0, 1)
+    ]
     gains_g = Gather(gx, g, (gx_s, gx_r), on_g)
     gains_z = Gather(gz, z, (gz_s, gz_r), on_z)
 
     pl.semaphore_wait(barrier, 3 * (N - 1))
 
     wo_chunk[1].start()
+    wo_chunk[0].start()
     inputs.start()
     loads["x0"].wait()
     xf = x0[...].astype(F32)
@@ -295,37 +303,16 @@
     loads["vw"].wait()
     for i in range(HALF // 128):
         rows = pl.ds(pl.multiple_of(HALF * near + 128 * i, 128), 128)
-        part = jnp.transpose(vw[1, rows, :].astype(F32))
+        part = jnp.transpose(vw[rows, :].astype(F32))
         gvt[:, 128 * i : 128 * i + 128] = (part * gain[1:2, rows]).astype(BF)
     swap_slice.start()
-    wo_chunk[0].start()
     swap_block.start()
-
-    loads["q"].wait()
-    loads["k"].wait()
-    causal = lax.broadcasted_iota(jnp.int32, (TOK, TOK), 0) <= lax.broadcasted_iota(jnp.int32, (TOK, TOK), 1)
-
-    def attend(l):
-        for h in (0, 1):
-            scores = nt(k[l], q[l, :, HD * h : HD * h + HD])
-            raised = jnp.where(causal, jnp.exp(50.0 * jnp.tanh(scores * (1.0 / 600.0))), 0.0)
-            probs[2 * l + h] = (raised / jnp.sum(raised, axis=0, keepdims=True)).astype(BF)
-
-    attend(1)
-    loads["wo"].wait()
-    loads["cot"].wait()
-    loads["x1"].wait()
-    dctx1 = nt(wo[1], cot[:, mine])
-
-    wo_chunk[1].wait()
-    wo_parts[1].start()
-    swap_slice.wait()
-    mz[z] = nt(mrx[...], wo[0]).astype(BF)
-    products.start()
-
     for i in range(D // 128):
         two = gain[:, 128 * i : 128 * i + 128]
         gcol[128 * i : 128 * i + 128, :] = jnp.transpose(jnp.concatenate([two, two, two, two], 0))
+
+    wo_chunk[1].wait()
+    wo_parts[1].start()
     own_rows = pl.ds(pl.multiple_of(FB * y, 32), FB)
 
     squares.wait()
@@ -335,43 +322,57 @@
         x0p[n] = jnp.concatenate([dwf[ROWS * n : ROWS * n + ROWS, :], jnp.zeros((48 - ROWS, TOK), F32)], 0).astype(BF)
     mixed.start()
 
+
+    loads["q"].wait()
+    loads["k"].wait()
+    causal = lax.broadcasted_iota(jnp.int32, (TOK, TOK), 0) <= lax.broadcasted_iota(jnp.int32, (TOK, TOK), 1)
+
+    def attend(l):
+        for h in (0, 1):
+            scores = nt(k[l], q[l, :, HD * h : HD * h + HD])
+            raised = jnp.where(causal, jnp.exp(50.0 * jnp.tanh(scores * (1.0 / 600.0))), 0.0)
+            probs[2 * l + h] = (raised / jnp.sum(raised, axis=0, keepdims=True)).astype(BF)
+
+    attend(1)
+    loads["wo1"].wait()
+    loads["cot"].wait()
+    dctx1 = nt(wo[1], cot[:, mine])
+    loads["wo0"].wait()
+    loads["x1"].wait()
+    swap_slice.wait()
+    mz[z] = nt(mrx[...], wo[0]).astype(BF)
+    products.start()
+
     wo_chunk[0].wait()
     wo_parts[0].start()
 
     inputs.relay()
-    wo_parts[1].wait()
-
-    def values(l, dctx):
-        return nt(probs[2 * l], dctx[0:HD]) + nt(probs[2 * l + 1], dctx[HD : 2 * HD])
-
-    dctx1 = (dctx1 + nt(wot[1].reshape(2 * HD, HALF), cot[:, other])).astype(BF)
-    dv = values(1, dctx1).astype(BF)
-    dvy[1, y] = dv
-    dva[1, g] = dv
-    heads[1].start()
-    group[1].start()
-    attend(0)
-
-    def regroup(part):
-        for b in range(N):
-            dwf[...] = part(b).astype(F32)
-            for n in range(N):
-                xnf[n, ROWS * b : ROWS * b + ROWS, :] = dwf[ROWS * n : ROWS * n + ROWS, :]
-
-    products.wait()
-    m_sum = mz[0:4].reshape(HD, 2 * HD).astype(F32) + mz[4:8].reshape(HD, 2 * HD).astype(F32)
-    mt[g] = jnp.transpose(m_sum).astype(BF)
-    maps.start()
-
+    wo_parts[1].pass_on()
     mixed.wait()
     for n in range(N):
         dwf[ROWS * n : ROWS * n + ROWS, :] = x0a[n].astype(F32)[0:ROWS]
     x0y[y] = dwf[...].astype(BF)
     mixed_y.start()
-
-    swap_block.wait()
-    blocks.start()
+    wo_parts[1].wait()
+
+    def values(l, dctx):
+        return nt(probs[2 * l], dctx[0:HD]) + nt(probs[2 * l + 1], dctx[HD : 2 * HD])
+
+    dctx1 = (dctx1 + nt(wot[1].reshape(2 * HD, HALF), cot[:, other])).astype(BF)
+    dv = values(1, dctx1).astype(BF)
+    dvy[1, y] = dv
+    dva[1, z] = dv
+    heads[1].start()
+    group[1].start()
+    products.wait()
+    m_sum = mz[0:4].reshape(HD, 2 * HD).astype(F32) + mz[4:8].reshape(HD, 2 * HD).astype(F32)
+    mt[g] = jnp.transpose(m_sum).astype(BF)
+    maps.start()
+
+
+    attend(0)
     wo_parts[0].pass_on()
+    maps.pass_on()
 
     inputs.wait()
     total = jnp.zeros((1, TOK), F32)
@@ -382,12 +383,12 @@
     total = jnp.zeros((1, TOK), F32)
     for b in range(N):
         xnb[b] = (xt[b].astype(F32) * inv1 * gcol[FB * b : FB * b + FB, 1:2]).astype(BF)
-        dxn = nt(vw[1, FB * b : FB * b + FB, :], dvy[1, y])
+        dxn = nt(vw[FB * b : FB * b + FB, :], dvy[1, y])
         total = total + jnp.sum(dxn * xnb[b].astype(F32), axis=0, keepdims=True)
     mm[1, y] = jnp.broadcast_to(total * (1.0 / D), (8, TOK))
     means[1].start()
-
-    maps.pass_on()
+    normed.start()
+
     wo_parts[0].wait()
     wo_other = wot[0].reshape(2 * HD, HALF)
     base = nt(wo[0], cot[:, mine]) + nt(wo_other, cot[:, other])
@@ -396,13 +397,12 @@
     xt_mine = jnp.where(first, xt_half[0], xt_half[1])
     xt_other = jnp.where(first, xt_half[1], xt_half[0])
     y1 = nn(wo[0], xt_mine) + nn(wo_other, xt_other)
-    regroup(lambda b: xnb[b])
-    for n in range(N):
-        xnp[n] = xnf[n].astype(BF)
-    normed.start()
+    heads[1].relay()
     mixed_y.relay()
 
     maps.wait()
+    swap_block.wait()
+    blocks.start()
     heads[1].wait()
 
     def over_heads(left, l):
@@ -457,29 +457,32 @@
         gx[g, l : l + 1, 0:FB] = row[0:1] * scale
         return xhat, dxn * gcol[own_rows, l : l + 1]
 
-    normed.wait()
-    group[1].wait()
-    weight_grad(1, lambda n: xna[n])
-    mixed_y.wait()
-    regroup(lambda b: x0y[b])
-    for n in range(N):
-        x0w[n] = xnf[n].astype(BF)
     gx[g] = jnp.zeros((8, 384), F32)
     blocks.wait()
     xhat, gg = input_grad(1, xt[y].astype(F32), inv1)
     cot_blk[...] = (cot_blk[...] + inv1 * (gg - xhat * mean1)).astype(BF).astype(F32)
-
-    group[0].wait()
-    weight_grad(0, lambda n: x0w[n])
 
     heads[0].wait()
     xhat, gg = input_grad(0, x0[...].astype(F32), inv0)
     gains_g.start()
     mm[0, y] = jnp.broadcast_to(jnp.sum(gg * xhat, axis=0, keepdims=True) * (1.0 / D), (8, TOK))
     means[0].start()
+    mixed_y.wait()
+    for b in range(N):
+        dwf[...] = x0y[b].astype(F32)
+        for n in range(N):
+            xnf[n, ROWS * b : ROWS * b + ROWS, :] = dwf[ROWS * n : ROWS * n + ROWS, :]
+    for n in range(N):
+        x0w[n] = xnf[n].astype(BF)
+    group[0].wait()
+    weight_grad(0, lambda n: x0w[n])
+
     gains_g.wait()
     gz[z] = sum_of(gx)
     gains_z.start()
+    normed.wait()
+    group[1].wait()
+    weight_grad(1, lambda n: xna[n])
 
     means[0].wait()
     out[...] = (cot_blk[...] + inv0 * (gg - xhat * sum_of(mm.at[0])[0:1, :])).astype(BF)
@@ -501,9 +504,9 @@
     out, weights, gains = pl.pallas_call(
         kernel,
         out_shape=(
-            jax.ShapeDtypeStruct((FB, TOK), BF),
-            jax.ShapeDtypeStruct((ROWS, 2, HD), F32),
-            jax.ShapeDtypeStruct((2, FB), F32),
+            vmem((FB, TOK), BF),
+            vmem((ROWS, 2, HD), F32),
+            vmem((2, FB), F32),
         ),
         in_specs=[hbm] * 7,
         out_specs=[pl.BlockSpec(memory_space=vmem)] * 3,
@@ -512,7 +515,7 @@
             vmem((2, D), F32),
             vmem((2, TOK, 2 * HD), BF),
             vmem((2, TOK, HD), BF),
-            vmem((2, D, HD), BF),
+            vmem((D, HD), BF),
             vmem((2, 2 * HD, HALF), BF),
             vmem((FB, TOK), BF),
             vmem((N, FB, TOK), BF),
@@ -531,7 +534,6 @@
             vmem((N, FB, TOK), BF),
             vmem((N, FB, TOK), F32),
             vmem((N, FB, TOK), BF),
-            vmem((N, FB, TOK), BF),
             vmem((2, N, TOK, HD), BF),
             vmem((2, N, TOK, HD), BF),
             vmem((N, 8, TOK), F32),
@@ -544,7 +546,7 @@
             vmem((TOK, 384), F32),
             vmem((FB, TOK), F32),
         ]
-        + [dma((8,))]
+        + [dma((9,))]
         + one
         + one
         + one

time: 72.7 us -> 67.8 us (0.933)
  Pallas kernels: 67.6 us -> 65.2 us
  local copies, waits for them, and re-layouts: 4.17 us -> 1.83 us
    pallas_call x1, Pallas kernels: 67.6 us -> 65.2 us  [body(): pl.pallas_call(kernel, out_shape=(vmem((FB, TOK), BF), vmem((ROWS, 2, HD)...]
    unnamed x3, local copies, waits for them, and re-layouts: 4.17 us -> 1.83 us
where the time goes in v4:
time: 67.8 us; the launch traced here: 67.6 us
  Pallas kernels  65.2 us (96%)
  local copies, waits for them, and re-layouts  1.83 us (3%)
    pallas_call x1, Pallas kernels, body(): pl.pallas_call(kernel, out_shape=(vmem((FB, TOK), BF), vmem((ROWS, 2, HD)...  65.2 us
    unnamed x3, local copies, waits for them, and re-layouts  1.83 us

profile of v4, /device:TPU:1, one launch (start us, length us, event | category | flops | bytes accessed | tf_op | source)
XLA Modules:
  0.0 67.6 jit_solution(15607376073404080934)
XLA Ops:
  0.6 65.2 %shard_map.94 = (bf16[288,128]{1,0:T(8,128)(2,1)S(1)}, f32[36,2,128]{2,1,0:T(2,128)S(1)}, f32[2,288]{1,0:T(2,128)S(1)}) custom-call(bf16[128,2304]{1,0:T(8,128)(2,1)} %cot_in.1, bf16[2,288,128]{2,1,0:T(8,128)(2,1)} %bitcast.5, f32[2,2304]{1,0:T(2,128)} %gain_in.1, bf16[2,128,256]{2,1,0:T(8,128)(2,1)} %q_in.1, bf16[2,128,128]{2,1,0:T(8,128)(2,1)} %k_in.1, ...), custom_call_target="tpu_custom_call" | custom-call | tf_op jit(solution)/shard_map/pallas_call | solution.py:504
  65.8 0.6 copy.13
  66.4 0.6 copy.14
  67.1 0.6 copy.15

commit v5 on v4

--- a/solution.py
+++ b/solution.py
@@ -231,6 +231,16 @@
         for item in under_way:
             item.sent()
 
+    barrier = pltpu.get_barrier_semaphore()
+
+    def hello(dev):
+        pl.semaphore_signal(barrier, inc=1, device_id=dev, device_id_type=MESH)
+
+    for n in FAR_FIRST:
+        hello(on_y(wrap(y + n)))
+        hello(on_z(wrap(z + n)))
+        hello(on_g(wrap(g + n)))
+
     loads = {}
     for n, (name, src, dst) in enumerate(
         [
@@ -240,16 +250,6 @@
     ):
         loads[name] = pltpu.make_async_copy(src, dst, in_r.at[n])
         loads[name].start()
-
-    barrier = pltpu.get_barrier_semaphore()
-
-    def hello(dev):
-        pl.semaphore_signal(barrier, inc=1, device_id=dev, device_id_type=MESH)
-
-    for n in FAR_FIRST:
-        hello(on_y(wrap(y + n)))
-        hello(on_z(wrap(z + n)))
-        hello(on_g(wrap(g + n)))
 
     shifts = tuple(c // 2 if c % 2 == 0 else (4 if c == 1 else 8 - c // 2) for c in range(N))
     shift = jnp.where(core == 0, g // 2, jnp.where(g == 1, 4, 8 - g // 2))
@@ -387,6 +387,7 @@
         total = total + jnp.sum(dxn * xnb[b].astype(F32), axis=0, keepdims=True)
     mm[1, y] = jnp.broadcast_to(total * (1.0 / D), (8, TOK))
     means[1].start()
+    heads[1].relay()
     normed.start()
 
     wo_parts[0].wait()
@@ -397,7 +398,6 @@
     xt_mine = jnp.where(first, xt_half[0], xt_half[1])
     xt_other = jnp.where(first, xt_half[1], xt_half[0])
     y1 = nn(wo[0], xt_mine) + nn(wo_other, xt_other)
-    heads[1].relay()
     mixed_y.relay()
 
     maps.wait()
@@ -418,8 +418,8 @@
     dv = values(0, dctx0).astype(BF)
     dvy[0, y] = dv
     dva[0, g] = dv
+    heads[0].start()
     group[0].start()
-    heads[0].start()
     blocks.pass_on()
 
     for b in range(N):
@@ -457,7 +457,7 @@
         gx[g, l : l + 1, 0:FB] = row[0:1] * scale
         return xhat, dxn * gcol[own_rows, l : l + 1]
 
-    gx[g] = jnp.zeros((8, 384), F32)
+    gx[g] = jnp.zeros((2, 384), F32)
     blocks.wait()
     xhat, gg = input_grad(1, xt[y].astype(F32), inv1)
     cot_blk[...] = (cot_blk[...] + inv1 * (gg - xhat * mean1)).astype(BF).astype(F32)
@@ -538,8 +538,8 @@
             vmem((2, N, TOK, HD), BF),
             vmem((N, 8, TOK), F32),
             vmem((2, N, 8, TOK), F32),
-            vmem((N, 8, 384), F32),
-            vmem((N, 8, 384), F32),
+            vmem((N, 2, 384), F32),
+            vmem((N, 2, 384), F32),
             vmem((FB, HD), F32),
             vmem((2, N, 40, HD), F32),
             vmem((2, N, 40, HD), F32),

time: 67.8 us -> 67.3 us (level)
  no operation moved by 1% of the time
where the time goes in v5:
time: 67.3 us; the launch traced here: 67.2 us
  Pallas kernels  64.7 us (96%)
  local copies, waits for them, and re-layouts  1.83 us (3%)
    pallas_call x1, Pallas kernels, body(): pl.pallas_call(kernel, out_shape=(vmem((FB, TOK), BF), vmem((ROWS, 2, HD)...  64.7 us
    unnamed x3, local copies, waits for them, and re-layouts  1.83 us

profile of v5, /device:TPU:1, one launch (start us, length us, event | category | flops | bytes accessed | tf_op | source)
XLA Modules:
  0.0 67.2 jit_solution(10497155340219547244)
XLA Ops:
  0.6 64.7 %shard_map.94 = (bf16[288,128]{1,0:T(8,128)(2,1)S(1)}, f32[36,2,128]{2,1,0:T(2,128)S(1)}, f32[2,288]{1,0:T(2,128)S(1)}) custom-call(bf16[128,2304]{1,0:T(8,128)(2,1)} %cot_in.1, bf16[2,288,128]{2,1,0:T(8,128)(2,1)} %bitcast.5, f32[2,2304]{1,0:T(2,128)} %gain_in.1, bf16[2,128,256]{2,1,0:T(8,128)(2,1)} %q_in.1, bf16[2,128,128]{2,1,0:T(8,128)(2,1)} %k_in.1, ...), custom_call_target="tpu_custom_call" | custom-call | tf_op jit(solution)/shard_map/pallas_call | solution.py:504
  65.3 0.6 copy.13
  66.0 0.6 copy.14
  66.6 0.6 copy.15
